TPU v7x, 128 devices: a whole 4x4x4 slice. The times are simulated.
128 devices in a mesh: row: 8 (over y_lo, x), col: 16 (over z, y_hi, core).
Axes of the slice: x: 4, y: 4 (y_hi: 2, y_lo: 2; y = y_hi * 2 + y_lo), z: 4, core: 2. Of those that a mesh axis runs over, the one named last changes fastest.
Arguments:
- latent: bfloat16 [192, 256, 1280], P('row', 'col'), may hold values from -6 to 6
- w_query: bfloat16 [1280, 1280], replicated, may hold values from -0.15625 to 0.15625
- w_key: bfloat16 [1280, 1280], replicated, may hold values from -0.15625 to 0.15625
- w_value: bfloat16 [1280, 1280], replicated, may hold values from -0.15625 to 0.15625
- w_out: bfloat16 [1280, 1280], replicated, may hold values from -0.15625 to 0.15625
- depth_kernel: float32 [9, 1280], replicated, may hold values from -2 to 2
- w_proj: bfloat16 [1280, 1280], replicated, may hold values from -0.15625 to 0.15625
Outputs:
- refined: bfloat16 [192, 256, 1280], P('row', 'col')
All inputs are finite; a program needn't handle non-finite values.
Results may differ from a plain program's by a relative error of at most 0.011.
Values may be sent and summed in bfloat16 or wider, within the bound.
No kernel may reach another device: no remote copies, remote signals or barrier semaphores. Data moves between devices by JAX's collectives and lax.ppermute only.
A program may use at most 128 MiB of HBM per device.

v0:
```python
import functools

import jax
import jax.numpy as jnp
import numpy as np
from jax import lax
from jax.experimental import pallas as pl
from jax.experimental.pallas import tpu as pltpu
from jax.sharding import PartitionSpec as P

D = 1280
HEADS = 20
HEAD = D // HEADS
GROUPS = 32
GROUP = D // GROUPS
M = 4
TH = 24
TW = 16
WH = TH + 2 * M
WW = TW + 2 * M
OWN = TH * TW
WIN = WH * WW
N_ROW = 8
N_COL = 16
DEV = N_ROW * N_COL
SENT = WH * TW
STRIP = WH * M
PART_H = TH // N_ROW
LANES = 256
BLOCKS = D // LANES
F32 = jnp.float32
BF16 = jnp.bfloat16
HIGH_SUM = 2.0**100
LOW_SUM = 2.0**-100


def window_matrix():
    out = np.zeros((WIN, WIN), np.float32)
    for w in range(WH):
        for c in range(WW):
            if c < M:
                src = SENT + w * M + c
            elif c < M + TW:
                src = w * TW + c - M
            else:
                src = SENT + STRIP + w * M + c - M - TW
            out[w * WW + c, src] = 1
    return out.astype(jnp.bfloat16)


def sending_matrix():
    out = np.zeros((SENT + 2 * STRIP, WIN), np.float32)
    for a in range(N_ROW):
        for k in range(WH // N_ROW):
            w = (a + M) % N_ROW + N_ROW * k
            for b in range(TW):
                out[(a * TW + b) * 4 + k, w * WW + M + b] = 1
            for b in range(M):
                out[SENT + (a * M + b) * 4 + k, w * WW + b] = 1
                out[SENT + STRIP + (a * M + b) * 4 + k, w * WW + M + TW + b] = 1
    return out.astype(jnp.bfloat16)


def returning_matrix():
    out = np.zeros((OWN, OWN), np.float32)
    for r in range(N_ROW):
        for c in range(N_COL):
            for i in range(PART_H):
                out[(r * N_COL + c) * PART_H + i, (r * PART_H + i) * TW + c] = 1
    return out.astype(jnp.bfloat16)


def gathering_matrix(row, col):
    cell = lax.broadcasted_iota(jnp.int32, (OWN, SENT), 0)
    sent = lax.broadcasted_iota(jnp.int32, (OWN, SENT), 1)
    i, c = cell // TW, cell % TW
    r2, c2, k = sent // (N_COL * 4), (sent // 4) % N_COL, sent % 4
    late = (row >= M).astype(jnp.int32)
    hit = jnp.logical_and(c == c2, i == PART_H * r2 + k - late)
    local_row = (i % PART_H) * N_ROW + row
    tile_row = i // PART_H
    two_rows = jnp.logical_or(
        jnp.logical_and(local_row < M, tile_row > 0),
        jnp.logical_and(local_row >= TH - M, tile_row < N_ROW - 1),
    )
    two_cols = jnp.logical_or(
        jnp.logical_and(col < M, c > 0),
        jnp.logical_and(col >= TW - M, c < N_COL - 1),
    )
    scale = jnp.where(two_rows, 0.5, 1.0) * jnp.where(two_cols, 0.5, 1.0)
    return jnp.where(hit, scale, 0.0).astype(BF16)


def dot(a, b):
    return jnp.dot(a, b, preferred_element_type=F32)


def three_parts(row):
    full = jnp.broadcast_to(row, (8, row.shape[1]))
    high = full.astype(BF16).astype(F32)
    rest = full - high
    mid = rest.astype(BF16).astype(F32)
    low = rest - mid
    which = lax.broadcasted_iota(jnp.int32, full.shape, 0)
    parts = jnp.where(which == 0, high, jnp.where(which == 1, mid, jnp.where(which == 2, low, 0.0)))
    return parts.astype(BF16)


def group_mean(row, count):
    chan = lax.broadcasted_iota(jnp.int32, (D, 128), 0)
    first = GROUP * lax.broadcasted_iota(jnp.int32, (D, 128), 1)
    member = jnp.where(jnp.logical_and(chan >= first, chan < first + GROUP), 1.0, 0.0).astype(BF16)
    sums = jnp.sum(dot(three_parts(row), member), axis=0, keepdims=True) * (1.0 / (GROUP * count))
    chan = lax.broadcasted_iota(jnp.int32, (128, D), 1)
    first = GROUP * lax.broadcasted_iota(jnp.int32, (128, D), 0)
    spread = jnp.where(jnp.logical_and(chan >= first, chan < first + GROUP), 1.0, 0.0).astype(BF16)
    return jnp.sum(dot(three_parts(sums), spread), axis=0, keepdims=True)


def group_stats(x_ref, cells):
    mean = group_mean(jnp.sum(x_ref[...], axis=0, keepdims=True), cells)
    var = group_mean(jnp.sum(jnp.square(x_ref[...] - mean), axis=0, keepdims=True), cells)
    return mean, 1.0 / jnp.sqrt(var + 1e-05)


def safe_head(j, pair, half, q_ref, k_ref, v_ref):
    lanes = pl.ds(pair * 128, 128)
    query = q_ref[j, :, lanes]
    lane = lax.broadcasted_iota(jnp.int32, query.shape, 1)
    query = jnp.where((lane // HEAD) == half, query.astype(F32), 0.0).astype(BF16)
    scores = lax.dot_general(
        query, k_ref[j, :, lanes], (((1,), (1,)), ((), ())), preferred_element_type=F32
    )
    expo = jnp.exp(scores - jnp.max(scores, axis=1, keepdims=True))
    probs = (expo / jnp.sum(expo, axis=1, keepdims=True)).astype(BF16)
    return dot(probs, v_ref[j, :, lanes])


def refine(rows, cols, x_ref, weights, buffers, sems, emit):
    cells = rows * cols
    wq, wk, wv, wo, taps, wp = weights
    wq_s, wk_s, wv_s, wo_s, wp_s, normed, q_ref, k_ref, v_ref, att, act, range_ref = buffers
    copies = [
        pltpu.make_async_copy(src, dst, sems.at[i])
        for i, (src, dst) in enumerate(
            ((wq, wq_s), (wk, wk_s), (wv, wv_s), (wo, wo_s), (wp, wp_s))
        )
    ]

    mean, rstd = group_stats(x_ref, cells)
    normed[...] = ((x_ref[...] - mean) * rstd).astype(BF16)
    for copy in copies[:3]:
        copy.wait()

    range_ref[0] = jnp.full((8, 128), 1.0, F32)
    range_ref[1] = jnp.full((8, 128), 1.0, F32)

    def heads(j, carry):
        block = pl.ds(pl.multiple_of(j * LANES, LANES), LANES)
        n = normed[...]
        q_ref[j] = (dot(n, wq_s[:, block]) * (1.0 / 8.0)).astype(BF16)
        k_ref[j] = dot(n, wk_s[:, block]).astype(BF16)
        v_ref[j] = dot(n, wv_s[:, block]).astype(BF16)
        lane = lax.broadcasted_iota(jnp.int32, (cells, 128), 1)
        low, high = range_ref[0], range_ref[1]
        for pair in range(2):
            lanes = slice(pair * 128, pair * 128 + 128)
            query = q_ref[j, :, lanes]
            key = k_ref[j, :, lanes]
            value = jnp.concatenate([v_ref[j, :, lanes], jnp.ones((cells, 128), BF16)], axis=1)
            done = []
            for half in range(2):
                mine = jnp.where((lane < HEAD) == (half == 0), query, jnp.zeros_like(query))
                scores = lax.dot_general(
                    mine, key, (((1,), (1,)), ((), ())), preferred_element_type=F32
                )
                out = dot(jnp.exp(scores).astype(BF16), value)
                total = out[:, 128:]
                low = jnp.minimum(low, jnp.min(total.reshape(cells // 8, 8, 128), axis=0))
                high = jnp.maximum(high, jnp.max(total.reshape(cells // 8, 8, 128), axis=0))
                done.append(out[:, :128] / total)
            att[:, pl.ds(pl.multiple_of(j * LANES + pair * 128, 128), 128)] = jnp.where(
                lane < HEAD, done[0], done[1]
            ).astype(BF16)
        range_ref[0] = low
        range_ref[1] = high
        return carry

    lax.fori_loop(0, BLOCKS, heads, 0)
    in_range = jnp.logical_and(jnp.min(range_ref[0]) > LOW_SUM, jnp.max(range_ref[1]) < HIGH_SUM)

    @pl.when(jnp.logical_not(in_range))
    def _():
        def again(j, carry):
            lane = lax.broadcasted_iota(jnp.int32, (cells, 128), 1)
            for pair in range(2):
                done = [safe_head(j, pair, half, q_ref, k_ref, v_ref) for half in range(2)]
                att[:, pl.ds(pl.multiple_of(j * LANES + pair * 128, 128), 128)] = jnp.where(
                    lane < HEAD, done[0], done[1]
                ).astype(BF16)
            return carry

        lax.fori_loop(0, BLOCKS, again, 0)

    copies[3].wait()
    for j in range(BLOCKS):
        block = slice(j * LANES, j * LANES + LANES)
        x_ref[:, block] += dot(att[...], wo_s[:, block])

    mean, rstd = group_stats(x_ref, cells)
    edge = jnp.zeros((cols, D), F32)
    act[pl.ds(0, cols), :] = edge
    act[pl.ds(cols + cells, cols), :] = edge
    chunk = 4 * cols

    def activate(i, carry):
        at = pl.ds(pl.multiple_of(i * chunk, chunk), chunk)
        value = (x_ref[at, :] - mean) * rstd
        act[pl.ds(pl.multiple_of(i * chunk + cols, 8), chunk), :] = value / (1.0 + jnp.exp(-value))
        return carry

    lax.fori_loop(0, rows // 4, activate, 0)

    def convolve(i, carry):
        spot = lax.broadcasted_iota(jnp.int32, (1, cols, 128), 1)
        start = pl.multiple_of(i * chunk, chunk)
        for t in range(D // 128):
            lanes = slice(t * 128, t * 128 + 128)
            lines = [act[pl.ds(start + d * cols, chunk), lanes] for d in range(3)]
            sums = []
            for dj in range(3):
                part = lines[0] * taps[dj : dj + 1, lanes]
                part = part + lines[1] * taps[3 + dj : 4 + dj, lanes]
                sums.append(part + lines[2] * taps[6 + dj : 7 + dj, lanes])
            left = pltpu.roll(sums[0], 1, 0).reshape(4, cols, 128)
            right = pltpu.roll(sums[2], chunk - 1, 0).reshape(4, cols, 128)
            mixed = sums[1].reshape(4, cols, 128)
            mixed = mixed + jnp.where(spot > 0, left, 0.0) + jnp.where(spot < cols - 1, right, 0.0)
            normed[pl.ds(start, chunk), lanes] = mixed.reshape(chunk, 128).astype(BF16)
        return carry

    lax.fori_loop(0, rows // 4, convolve, 0)
    copies[4].wait()
    for j in range(BLOCKS):
        block = slice(j * LANES, j * LANES + LANES)
        emit(block, x_ref[:, block] + dot(normed[...], wp_s[:, block]))


def start_weights(weights, buffers, sems):
    for i, w in enumerate((0, 1, 2, 3, 5)):
        pltpu.make_async_copy(weights[w], buffers[i], sems.at[i]).start()


def tile_kernel(
    above, own, below, left, right, window, sending, wq, wk, wv, wo, taps, wp,
    main, to_left, to_right, parts, x_ref, out, part_sems, sems, *buffers,
):
    pieces = (above, own, below, left, right)
    copies, start = [], 0
    for i, piece in enumerate(pieces):
        copies.append(
            pltpu.make_async_copy(piece, parts.at[pl.ds(start, piece.shape[0])], part_sems.at[i])
        )
        start += piece.shape[0]
    for copy in copies:
        copy.start()
    weights = (wq, wk, wv, wo, taps, wp)
    start_weights(weights, buffers, sems)
    for copy in copies:
        copy.wait()
    for j in range(BLOCKS):
        block = slice(j * LANES, j * LANES + LANES)
        x_ref[:, block] = dot(window[...], parts[:, block])

    def emit(block, values):
        out[:, block] = values.astype(BF16)

    refine(WH, WW, x_ref, weights, buffers, sems, emit)
    for j in range(BLOCKS):
        block = slice(j * LANES, j * LANES + LANES)
        sent = dot(sending[...], out[:, block]).astype(BF16)
        main[:, block] = sent[:SENT]
        to_left[:, block] = sent[SENT : SENT + STRIP]
        to_right[:, block] = sent[SENT + STRIP :]


def sub_kernel(
    got, gathering, returning, wq, wk, wv, wo, taps, wp,
    result, local, x_ref, out, sems, *buffers,
):
    weights = (wq, wk, wv, wo, taps, wp)
    start_weights(weights, buffers, sems)
    for j in range(BLOCKS):
        block = slice(j * LANES, j * LANES + LANES)
        value = dot(gathering[...], got[:, block]).astype(BF16)
        local[:, block] = value
        x_ref[:, block] = value.astype(F32)

    def emit(block, values):
        dilated = values.astype(BF16).astype(F32)
        out[:, block] = (0.6 * local[:, block].astype(F32) + 0.4 * dilated).astype(BF16)

    refine(TH, TW, x_ref, weights, buffers, sems, emit)
    for j in range(BLOCKS):
        block = slice(j * LANES, j * LANES + LANES)
        result[:, block] = dot(returning[...], out[:, block]).astype(BF16)


def scratch(cells, cols):
    square = pltpu.VMEM((D, D), BF16)
    heads = pltpu.VMEM((BLOCKS, cells, LANES), BF16)
    return [
        pltpu.SemaphoreType.DMA((5,)),
        square, square, square, square, square,
        pltpu.VMEM((cells, D), BF16),
        heads, heads, heads,
        pltpu.VMEM((cells, D), BF16),
        pltpu.VMEM((cells + 2 * cols, D), F32),
        pltpu.VMEM((2, 8, 128), F32),
    ]


ANY = pl.BlockSpec(memory_space=pl.ANY)
VMEM = pl.BlockSpec(memory_space=pltpu.VMEM)
PARAMS = dict(vmem_limit_bytes=56 * 2**20)


def tile_block(above, own, below, left, right, weights):
    rows = jax.ShapeDtypeStruct
    return pl.pallas_call(
        tile_kernel,
        out_shape=(rows((SENT, D), BF16), rows((STRIP, D), BF16), rows((STRIP, D), BF16)),
        in_specs=[ANY] * 5 + [VMEM] * 2 + [ANY] * 4 + [VMEM, ANY],
        out_specs=(VMEM, VMEM, VMEM),
        scratch_shapes=[
            pltpu.VMEM((WIN, D), BF16),
            pltpu.VMEM((WIN, D), F32),
            pltpu.VMEM((WIN, D), BF16),
            pltpu.SemaphoreType.DMA((5,)),
            *scratch(WIN, WW),
        ],
        compiler_params=pltpu.CompilerParams(**PARAMS),
        name="tile_block",
    )(above, own, below, left, right, window_matrix(), sending_matrix(), *weights)


def sub_block(got, gathering, weights):
    return pl.pallas_call(
        sub_kernel,
        out_shape=jax.ShapeDtypeStruct((OWN, D), BF16),
        in_specs=[VMEM] * 3 + [ANY] * 4 + [VMEM, ANY],
        out_specs=VMEM,
        scratch_shapes=[
            pltpu.VMEM((OWN, D), BF16),
            pltpu.VMEM((OWN, D), F32),
            pltpu.VMEM((OWN, D), BF16),
            *scratch(OWN, TW),
        ],
        compiler_params=pltpu.CompilerParams(**PARAMS),
        name="sub_block",
    )(got, gathering, returning_matrix(), *weights)


def shift(value, axis, step):
    count = lax.axis_size(axis)
    pairs = [(i, i + step) for i in range(count) if 0 <= i + step < count]
    return lax.ppermute(value, axis, pairs)


def body(latent, w_query, w_key, w_value, w_out, depth_kernel, w_proj):
    weights = (w_query, w_key, w_value, w_out, depth_kernel, w_proj)
    row, col = lax.axis_index("row"), lax.axis_index("col")
    gathering = gathering_matrix(row, col)
    above = shift(latent[TH - M :], "row", 1)
    below = shift(latent[:M], "row", -1)
    tall = jnp.concatenate([above, latent, below], axis=0)
    left = shift(tall[:, TW - M :].reshape(STRIP, D), "col", 1)
    right = shift(tall[:, :M].reshape(STRIP, D), "col", -1)
    main, to_left, to_right = tile_block(
        above.reshape(M * TW, D), latent.reshape(OWN, D), below.reshape(M * TW, D),
        left, right, weights,
    )
    from_right = shift(to_left, "col", -1).reshape(N_ROW, M, 4, D).astype(F32)
    from_left = shift(to_right, "col", 1).reshape(N_ROW, M, 4, D).astype(F32)
    main = main.reshape(N_ROW, TW, 4, D).astype(F32)
    main = jnp.concatenate(
        [main[:, :M] + from_left, main[:, M : TW - M], main[:, TW - M :] + from_right], axis=1
    ).astype(BF16)
    both = functools.partial(
        lax.all_to_all, axis_name=("row", "col"), split_axis=0, concat_axis=0, tiled=True
    )
    got = both(main.reshape(DEV, 4, D)).reshape(SENT, D)
    refined = sub_block(got, gathering, weights)
    back = both(refined.reshape(DEV, 30, 128)).reshape(N_ROW, N_COL, PART_H, D)
    return back.transpose(2, 0, 1, 3).reshape(TH, TW, D)


def solution(mesh):
    return jax.shard_map(
        body,
        mesh=mesh,
        in_specs=(P("row", "col", None), P(), P(), P(), P(), P(), P()),
        out_specs=P("row", "col", None),
        check_vma=False,
    )
```

profile of v0, /device:TPU:1, one launch (start us, length us, event | category | flops | bytes accessed | tf_op | source)
XLA Modules:
  0.0 178.8 jit_solution(16006460100417998309)
XLA Ops:
  0.0 1.1 fusion.31
  1.1 4.0 %collective-permute-start = (bf16[4,16,1280]{2,1,0:T(8,128)(2,1)S(1)}, bf16[4,16,1280]{2,1,0:T(8,128)(2,1)S(1)}, u32[]{:S(2)}, u32[]{:S(2)}) collective-permute-start(bf16[4,16,1280]{2,1,0:T(8,128)(2,1)S(1)} %get-tuple-element.16), channel_id=1, source_target_pairs={{0,16},{16,32},{32,48},{48,64},{64,80},{80,96},{96,112},{1,17},{17... | collective-permute-start | bytes 491528 | tf_op jit(solution)/shard_map/ppermute | solution.py:367
  5.1 1.3 collective-permute-start.1
  6.4 1.5 collective-permute-done
  8.0 3.7 %collective-permute-done.1 = bf16[4,16,1280]{2,1,0:T(8,128)(2,1)S(1)} collective-permute-done((bf16[4,16,1280]{2,1,0:T(8,128)(2,1)S(1)}, bf16[4,16,1280]{2,1,0:T(8,128)(2,1)S(1)}, u32[]{:S(2)}, u32[]{:S(2)}) %collective-permute-start.1) | collective-permute-done | bytes 163872 | tf_op jit(solution)/shard_map/ppermute | solution.py:367
  12.1 6.6 %collective-permute-start.2 = (bf16[128,1280]{1,0:T(8,128)(2,1)S(1)}, bf16[128,1280]{1,0:T(8,128)(2,1)S(1)}, u32[]{:S(2)}, u32[]{:S(2)}) collective-permute-start(bf16[128,1280]{1,0:T(8,128)(2,1)S(1)} %reshape.42), channel_id=1, source_target_pairs={{0,1},{1,2},{2,3},{3,4},{4,5},{5,6},{6,7},{7,8},{8,9},{9,10},{10,1... | collective-permute-start | bytes 983048 | tf_op jit(solution)/shard_map/ppermute | solution.py:367
  18.8 1.9 %collective-permute-start.3 = (bf16[128,1280]{1,0:T(8,128)(2,1)S(1)}, bf16[128,1280]{1,0:T(8,128)(2,1)S(1)}, u32[]{:S(2)}, u32[]{:S(2)}) collective-permute-start(bf16[128,1280]{1,0:T(8,128)(2,1)S(1)} %reshape.43), channel_id=1, source_target_pairs={{1,0},{2,1},{3,2},{4,3},{5,4},{6,5},{7,6},{8,7},{9,8},{10,9},{11,1... | collective-permute-start | bytes 983048 | tf_op jit(solution)/shard_map/ppermute | solution.py:367
  20.7 2.0 %collective-permute-done.2.left = bf16[128,1280]{1,0:T(8,128)(2,1)S(1)} collective-permute-done((bf16[128,1280]{1,0:T(8,128)(2,1)S(1)}, bf16[128,1280]{1,0:T(8,128)(2,1)S(1)}, u32[]{:S(2)}, u32[]{:S(2)}) %collective-permute-start.2) | collective-permute-done | bytes 327712 | tf_op jit(solution)/shard_map/ppermute | solution.py:367
  22.7 6.0 %collective-permute-done.3.right = bf16[128,1280]{1,0:T(8,128)(2,1)S(1)} collective-permute-done((bf16[128,1280]{1,0:T(8,128)(2,1)S(1)}, bf16[128,1280]{1,0:T(8,128)(2,1)S(1)}, u32[]{:S(2)}, u32[]{:S(2)}) %collective-permute-start.3) | collective-permute-done | bytes 327712 | tf_op jit(solution)/shard_map/ppermute | solution.py:367
  29.4 46.9 %tile_block.1 = (bf16[512,1280]{1,0:T(8,128)(2,1)}, bf16[128,1280]{1,0:T(8,128)(2,1)}, bf16[128,1280]{1,0:T(8,128)(2,1)}) custom-call(bf16[64,1280]{1,0:T(8,128)(2,1)} %bitcast.8, bf16[384,1280]{1,0:T(8,128)(2,1)} %bitcast.6, bf16[64,1280]{1,0:T(8,128)(2,1)} %bitcast.9, bf16[128,1280]{1,0:T(8,128)(2,1)} %copy-done.4, bf16[128,1280]{1,0:T(8,128)(2,1)} %copy-done.5, ...), custom_call_target="tpu_custom_call" | custom-call | tf_op jit(solution)/shard_map/tile_block/pallas_call | solution.py:330
  76.3 1.9 %collective-permute-start.4 = (bf16[128,1280]{1,0:T(8,128)(2,1)}, bf16[128,1280]{1,0:T(8,128)(2,1)S(1)}, u32[]{:S(2)}, u32[]{:S(2)}) collective-permute-start(bf16[128,1280]{1,0:T(8,128)(2,1)} %get-tuple-element.9), channel_id=1, source_target_pairs={{0,1},{1,2},{2,3},{3,4},{4,5},{5,6},{6,7},{7,8},{8,9},{9,10},{10,1... | collective-permute-start | bytes 983048 | tf_op jit(solution)/shard_map/ppermute | solution.py:367
  78.3 2.4 %collective-permute-start.5 = (bf16[128,1280]{1,0:T(8,128)(2,1)}, bf16[128,1280]{1,0:T(8,128)(2,1)S(1)}, u32[]{:S(2)}, u32[]{:S(2)}) collective-permute-start(bf16[128,1280]{1,0:T(8,128)(2,1)} %get-tuple-element.10), channel_id=1, source_target_pairs={{1,0},{2,1},{3,2},{4,3},{5,4},{6,5},{7,6},{8,7},{9,8},{10,9},{11,1... | collective-permute-start | bytes 983048 | tf_op jit(solution)/shard_map/ppermute | solution.py:367
  80.7 2.6 %convert_element_type.29 = bf16[8,16,4,1280]{3,2,1,0:T(4,128)(2,1)S(1)} reshape(bf16[512,1280]{1,0:T(8,128)(2,1)} %get-tuple-element.8) | data formatting | bytes 2621440 | tf_op jit(solution)/shard_map/convert_element_type | solution.py:385
  83.3 1.9 %convert_element_type.30 = f32[8,16,4,1280]{3,2,1,0:T(4,128)} convert(bf16[8,16,4,1280]{3,2,1,0:T(4,128)(2,1)S(1)} %convert_element_type.29) | non-fusion elementwise | flops 655360 | bytes 3932160 | tf_op jit(solution)/shard_map/convert_element_type | solution.py:385
  85.4 3.4 %collective-permute-done.5 = bf16[128,1280]{1,0:T(8,128)(2,1)S(1)} collective-permute-done((bf16[128,1280]{1,0:T(8,128)(2,1)}, bf16[128,1280]{1,0:T(8,128)(2,1)S(1)}, u32[]{:S(2)}, u32[]{:S(2)}) %collective-permute-start.5) | collective-permute-done | bytes 327712 | tf_op jit(solution)/shard_map/ppermute | solution.py:367
  88.9 1.7 fusion.15
  90.6 2.0 %pad_maximum_fusion = bf16[8,16,4,1280]{3,2,1,0:T(4,128)(2,1)} fusion(bf16[8,4,4,1280]{3,2,1,0:T(4,128)(2,1)S(1)} %get-tuple-element.12, bf16[8,8,4,1280]{3,2,1,0:T(4,128)(2,1)S(1)} %slice-done, bf16[8,4,4,1280]{3,2,1,0:T(4,128)(2,1)S(1)} %get-tuple-element.11), kind=kLoop, calls=%fused_computation.14 | loop fusion | flops 1310720 | bytes 2621440 | tf_op jit(solution)/shard_map/concatenate | solution.py:386
  92.6 11.4 %all-to-all-start = ((bf16[128,4,1280]{2,1,0:T(4,128)(2,1)}), bf16[128,4,1280]{2,1,0:T(4,128)(2,1)S(1)}, u32[]{:S(2)}, u32[]{:S(2)}) async-start(bf16[128,4,1280]{2,1,0:T(4,128)(2,1)} %bitcast.3), calls=%async_computation | async-start | bytes 2621440 | tf_op jit(solution)/shard_map/all_to_all | solution.py:392
  104.1 1.8 %select_convert_fusion.gathering = bf16[384,512]{1,0:T(8,128)(2,1)} fusion(s32[]{:T(128)S(6)} %axis_index.23, s32[]{:T(128)S(6)} %convert_element_type.36, s32[512]{0:T(512)S(1)} %get-tuple-element.18, s32[512]{0:T(512)S(1)} %get-tuple-element.20, s32[512]{0:T(512)S(1)} %get-tuple-element.19, s32[512]{0:T(512)S(1)} %get-tuple-element.29, ...), kind=kLoop, calls=%fused_computation.22 | loop fusion | flops 10420224 | bytes 413962 | tf_op jit(solution)/shard_map/convert_element_type | solution.py:91
  106.0 20.0 %all-to-all-done = bf16[128,4,1280]{2,1,0:T(4,128)(2,1)S(1)} async-done(((bf16[128,4,1280]{2,1,0:T(4,128)(2,1)}), bf16[128,4,1280]{2,1,0:T(4,128)(2,1)S(1)}, u32[]{:S(2)}, u32[]{:S(2)}) %all-to-all-start) | async-done | bytes 1310752 | tf_op jit(solution)/shard_map/all_to_all | solution.py:392
  126.0 1.2 reshape.44.got
  127.2 24.3 %sub_block.1 = bf16[384,1280]{1,0:T(8,128)(2,1)} custom-call(bf16[512,1280]{1,0:T(8,128)(2,1)} %reshape.44.got, bf16[384,512]{1,0:T(8,128)(2,1)} %select_convert_fusion.gathering, bf16[384,384]{1,0:T(8,128)(2,1)} %constant.119.clone.returning, bf16[1280,1280]{1,0:T(8,128)(2,1)} %wq.3, bf16[1280,1280]{1,0:T(8,128)(2,1)} %wk.3, bf16[1280,1280]{1,0:T(8,128)(2,1)} %wv.3, ...), custom_call_target="tpu_custom_call" | custom-call | tf_op jit(solution)/shard_map/sub_block/pallas_call | solution.py:348
  151.5 2.3 %reshape.45 = bf16[128,30,128]{2,1,0:T(8,128)(2,1)S(1)} reshape(bf16[384,1280]{1,0:T(8,128)(2,1)} %sub_block.1) | data formatting | bytes 1966080 | tf_op jit(solution)/shard_map/reshape | solution.py:394
  153.8 23.5 %all_to_all.10 = bf16[128,30,128]{2,1,0:T(8,128)(2,1)S(1)} all-to-all(bf16[128,30,128]{2,1,0:T(8,128)(2,1)S(1)} %reshape.45), channel_id=1, replica_groups=mesh['row'=8,'col'=16] {'row','col'}, dimensions={0} | all-to-all | bytes 1966080 | tf_op jit(solution)/shard_map/all_to_all | solution.py:394
  (33 shorter events, 3.2 us)
Async XLA Ops:
  0.0 7.9 %copy-start.1 = (bf16[24,16,1280]{2,1,0:T(8,128)(2,1)S(1)}, bf16[24,16,1280]{2,1,0:T(8,128)(2,1)}, u32[]{:S(2)}) copy-start(bf16[24,16,1280]{2,1,0:T(8,128)(2,1)} %param.10) | copy-start | bytes 2949124
  1.1 6.8 %collective-permute-start = (bf16[4,16,1280]{2,1,0:T(8,128)(2,1)S(1)}, bf16[4,16,1280]{2,1,0:T(8,128)(2,1)S(1)}, u32[]{:S(2)}, u32[]{:S(2)}) collective-permute-start(bf16[4,16,1280]{2,1,0:T(8,128)(2,1)S(1)} %get-tuple-element.16), channel_id=1, source_target_pairs={{0,16},{16,32},{32,48},{48,64},{64,80},{80,96},{96,112},{1,17},{17... | collective-permute-start | bytes 491528 | tf_op jit(solution)/shard_map/ppermute | solution.py:367
  5.1 6.6 %collective-permute-start.1 = (bf16[4,16,1280]{2,1,0:T(8,128)(2,1)S(1)}, bf16[4,16,1280]{2,1,0:T(8,128)(2,1)S(1)}, u32[]{:S(2)}, u32[]{:S(2)}) collective-permute-start(bf16[4,16,1280]{2,1,0:T(8,128)(2,1)S(1)} %get-tuple-element.15), channel_id=1, source_target_pairs={{16,0},{32,16},{48,32},{64,48},{80,64},{96,80},{112,96},{17,1},{33... | collective-permute-start | bytes 491528 | tf_op jit(solution)/shard_map/ppermute | solution.py:367
  7.9 4.1 %copy-start.2 = (bf16[4,16,1280]{2,1,0:T(8,128)(2,1)}, bf16[4,16,1280]{2,1,0:T(8,128)(2,1)S(1)}, u32[]{:S(2)}) copy-start(bf16[4,16,1280]{2,1,0:T(8,128)(2,1)S(1)} %collective-permute-done) | copy-start | bytes 491524
  11.7 7.0 %copy-start.3 = (bf16[4,16,1280]{2,1,0:T(8,128)(2,1)}, bf16[4,16,1280]{2,1,0:T(8,128)(2,1)S(1)}, u32[]{:S(2)}) copy-start(bf16[4,16,1280]{2,1,0:T(8,128)(2,1)S(1)} %collective-permute-done.1) | copy-start | bytes 491524
  12.1 10.6 %collective-permute-start.2 = (bf16[128,1280]{1,0:T(8,128)(2,1)S(1)}, bf16[128,1280]{1,0:T(8,128)(2,1)S(1)}, u32[]{:S(2)}, u32[]{:S(2)}) collective-permute-start(bf16[128,1280]{1,0:T(8,128)(2,1)S(1)} %reshape.42), channel_id=1, source_target_pairs={{0,1},{1,2},{2,3},{3,4},{4,5},{5,6},{6,7},{7,8},{8,9},{9,10},{10,1... | collective-permute-start | bytes 983048 | tf_op jit(solution)/shard_map/ppermute | solution.py:367
  18.8 9.9 %collective-permute-start.3 = (bf16[128,1280]{1,0:T(8,128)(2,1)S(1)}, bf16[128,1280]{1,0:T(8,128)(2,1)S(1)}, u32[]{:S(2)}, u32[]{:S(2)}) collective-permute-start(bf16[128,1280]{1,0:T(8,128)(2,1)S(1)} %reshape.43), channel_id=1, source_target_pairs={{1,0},{2,1},{3,2},{4,3},{5,4},{6,5},{7,6},{8,7},{9,8},{10,9},{11,1... | collective-permute-start | bytes 983048 | tf_op jit(solution)/shard_map/ppermute | solution.py:367
  22.7 6.0 %copy-start.4 = (bf16[128,1280]{1,0:T(8,128)(2,1)}, bf16[128,1280]{1,0:T(8,128)(2,1)S(1)}, u32[]{:S(2)}) copy-start(bf16[128,1280]{1,0:T(8,128)(2,1)S(1)} %collective-permute-done.2.left) | copy-start | bytes 983044
  28.7 0.7 copy-start.5
  76.3 8.9 %collective-permute-start.4 = (bf16[128,1280]{1,0:T(8,128)(2,1)}, bf16[128,1280]{1,0:T(8,128)(2,1)S(1)}, u32[]{:S(2)}, u32[]{:S(2)}) collective-permute-start(bf16[128,1280]{1,0:T(8,128)(2,1)} %get-tuple-element.9), channel_id=1, source_target_pairs={{0,1},{1,2},{2,3},{3,4},{4,5},{5,6},{6,7},{7,8},{8,9},{9,10},{10,1... | collective-permute-start | bytes 983048 | tf_op jit(solution)/shard_map/ppermute | solution.py:367
  78.3 10.5 %collective-permute-start.5 = (bf16[128,1280]{1,0:T(8,128)(2,1)}, bf16[128,1280]{1,0:T(8,128)(2,1)S(1)}, u32[]{:S(2)}, u32[]{:S(2)}) collective-permute-start(bf16[128,1280]{1,0:T(8,128)(2,1)} %get-tuple-element.10), channel_id=1, source_target_pairs={{1,0},{2,1},{3,2},{4,3},{5,4},{6,5},{7,6},{8,7},{9,8},{10,9},{11,1... | collective-permute-start | bytes 983048 | tf_op jit(solution)/shard_map/ppermute | solution.py:367
  83.3 1.9 %copy-start = (bf16[8,16,4,1280]{3,2,1,0:T(4,128)(2,1)}, bf16[8,16,4,1280]{3,2,1,0:T(4,128)(2,1)S(1)}, u32[]{:S(2)}) copy-start(bf16[8,16,4,1280]{3,2,1,0:T(4,128)(2,1)S(1)} %convert_element_type.29) | copy-start | bytes 3932164
  88.9 1.7 slice-start
  92.6 33.4 %all-to-all-start = ((bf16[128,4,1280]{2,1,0:T(4,128)(2,1)}), bf16[128,4,1280]{2,1,0:T(4,128)(2,1)S(1)}, u32[]{:S(2)}, u32[]{:S(2)}) async-start(bf16[128,4,1280]{2,1,0:T(4,128)(2,1)} %bitcast.3), calls=%async_computation | async-start | bytes 2621440 | tf_op jit(solution)/shard_map/all_to_all | solution.py:392
where the time goes:
time: 179 us
  Pallas kernels  71.2 us (40%)
  waiting for transfers between devices  36.6 us (20%)
  starting transfers between devices  29.5 us (16%)
  blocking collectives  23.5 us (13%)
  local copies, waits for them, and re-layouts  10.3 us (6%)
  other arithmetic  7.44 us (4%)
    pallas_call x1, Pallas kernels, tile_block(): pl.pallas_call(tile_kernel, out_shape=(rows((SENT, D), BF16), rows((STRIP...  46.9 us
    pallas_call x1, Pallas kernels, sub_block(): pl.pallas_call(sub_kernel, out_shape=jax.ShapeDtypeStruct((OWN, D), BF16)...  24.3 us
    all_to_all x1, blocking collectives, body(): back = both(refined.reshape(DEV, 30, 128)).reshape(N_ROW, N_COL, PART_H, D)  23.5 us
    all_to_all x1, waiting for transfers between devices, body(): got = both(main.reshape(DEV, 4, D)).reshape(SENT, D)  20 us
    ppermute x6, starting transfers between devices, shift(): return lax.ppermute(value, axis, pairs)  18.1 us
    ppermute x6, waiting for transfers between devices, shift(): return lax.ppermute(value, axis, pairs)  16.6 us
    all_to_all x1, starting transfers between devices, body(): got = both(main.reshape(DEV, 4, D)).reshape(SENT, D)  11.4 us
  transfers between devices with their start and end apart: 7, of which 6 were waited for; matrix products, arithmetic and copies ran while one was open for 4% of the time, Pallas kernels for 0%

commit v1 on v0

v1 whole, which is shorter than its diff:
```python
import functools

import jax
import jax.numpy as jnp
import numpy as np
from jax import lax
from jax.experimental import pallas as pl
from jax.experimental.pallas import tpu as pltpu
from jax.sharding import PartitionSpec as P

D = 1280
HEADS = 20
HEAD = D // HEADS
GROUPS = 32
GROUP = D // GROUPS
M = 4
TH = 24
TW = 16
WH = TH + 2 * M
WW = TW + 2 * M
OWN = TH * TW
WIN = WH * WW
N_ROW = 8
N_COL = 16
DEV = N_ROW * N_COL
SENT = WH * TW
STRIP = WH * M
SIDE = 2 * STRIP
PART_H = TH // N_ROW
LANES = 256
BLOCKS = D // LANES
F32 = jnp.float32
BF16 = jnp.bfloat16
HIGH_SUM = 2.0**100
LOW_SUM = 2.0**-100


def side_matrix():
    out = np.zeros((SIDE, SIDE), np.float32)
    for w in range(WH):
        for c in range(M):
            out[w * 8 + c, STRIP + w * M + c] = 1
            out[w * 8 + M + c, w * M + c] = 1
    return out.astype(jnp.bfloat16)


def main_matrix():
    out = np.zeros((128, 128), np.float32)
    for b in range(TW):
        for h in range(2):
            for k in range(4):
                out[b * 8 + h * 4 + k, h * 64 + k * TW + b] = 1
    return out.astype(jnp.bfloat16)


def strip_matrix():
    out = np.zeros((64, 64), np.float32)
    for b in range(M):
        for h in range(2):
            for k in range(4):
                out[b * 8 + h * 4 + k, h * 32 + k * 8 + b] = 1
                out[32 + b * 8 + h * 4 + k, h * 32 + k * 8 + M + b] = 1
    return out.astype(jnp.bfloat16)


def gather_matrices():
    out = np.zeros((2, 3, 2, 96, 256), np.float32)
    for late in range(2):
        for kind in range(3):
            for edge in range(2):
                for h in range(2):
                    for i in range(PART_H):
                        for c in range(N_COL):
                            two_cols = (kind == 0 and c > 0) or (kind == 2 and c < N_COL - 1)
                            shared = i == (2 if late else 0) and not edge
                            scale = (0.5 if two_cols else 1.0) * (0.5 if shared else 1.0)
                            to = h * 48 + i * TW + c
                            out[late, kind, edge, to, c * 8 + h * 4 + i + late] = scale
                            if shared:
                                out[late, kind, edge, to, 128 + c * 8 + h * 4 + (0 if late else 3)] = scale
    return out.reshape(6, 2, 96, 256).astype(jnp.bfloat16)


def packing_matrix():
    out = np.zeros((256, 240), np.float32)
    for t in range(5):
        for i in range(PART_H):
            for c in range(N_COL):
                at = 10 * i + 2 * t
                out[(at % 4) // 2 * 128 + c * 8 + at // 4, t * 48 + i * TW + c] = 1
    return out.astype(jnp.bfloat16)


def dot(a, b):
    return jnp.dot(a, b, preferred_element_type=F32)


def three_parts(row):
    full = jnp.broadcast_to(row, (8, row.shape[1]))
    high = full.astype(BF16).astype(F32)
    rest = full - high
    mid = rest.astype(BF16).astype(F32)
    low = rest - mid
    which = lax.broadcasted_iota(jnp.int32, full.shape, 0)
    parts = jnp.where(which == 0, high, jnp.where(which == 1, mid, jnp.where(which == 2, low, 0.0)))
    return parts.astype(BF16)


def group_matrices(member, spread):
    for ref, chan_axis in ((member, 0), (spread, 1)):
        chan = lax.broadcasted_iota(jnp.int32, ref.shape, chan_axis)
        first = GROUP * lax.broadcasted_iota(jnp.int32, ref.shape, 1 - chan_axis)
        inside = jnp.logical_and(chan >= first, chan < first + GROUP)
        ref[...] = jnp.where(inside, 1.0, 0.0).astype(BF16)


def group_mean(row, count, member, spread):
    sums = jnp.sum(dot(three_parts(row), member[...]), axis=0, keepdims=True) * (1.0 / (GROUP * count))
    return jnp.sum(dot(three_parts(sums), spread[...]), axis=0, keepdims=True)


def group_stats(x_ref, member, spread):
    cells = x_ref.shape[0]
    mean = group_mean(jnp.sum(x_ref[...], axis=0, keepdims=True), cells, member, spread)
    var = group_mean(jnp.sum(jnp.square(x_ref[...] - mean), axis=0, keepdims=True), cells, member, spread)
    return mean, 1.0 / jnp.sqrt(var + 1e-05)


def safe_head(j, pair, half, q_ref, k_ref, v_ref):
    lanes = pl.ds(pair * 128, 128)
    query = q_ref[j, :, lanes]
    lane = lax.broadcasted_iota(jnp.int32, query.shape, 1)
    query = jnp.where((lane // HEAD) == half, query.astype(F32), 0.0).astype(BF16)
    scores = lax.dot_general(
        query, k_ref[j, :, lanes], (((1,), (1,)), ((), ())), preferred_element_type=F32
    )
    expo = jnp.exp(scores - jnp.max(scores, axis=1, keepdims=True))
    probs = (expo / jnp.sum(expo, axis=1, keepdims=True)).astype(BF16)
    return dot(probs, v_ref[j, :, lanes])


def weight_copies(weights, buffers, sems):
    wq, wk, wv, wo, _, wp = weights

    def block(i, j):
        src = (wq, wk, wv)[i]
        return pltpu.make_async_copy(
            src.at[:, pl.ds(pl.multiple_of(j * LANES, LANES), LANES)], buffers[i].at[j], sems.at[i, j]
        )

    last = [
        pltpu.make_async_copy(wo, buffers[3], sems.at[3, 0]),
        pltpu.make_async_copy(wp, buffers[4], sems.at[4, 0]),
    ]
    return block, last


def start_block(weights, buffers, sems, j):
    block, _ = weight_copies(weights, buffers, sems)
    for i in range(3):
        block(i, j).start()


def refine(rows, side, x_ref, weights, buffers, sems, emit):
    cells = x_ref.shape[0]
    middle = rows * TW
    taps = weights[4]
    wq_s, wk_s, wv_s, wo_s, wp_s, normed, q_ref, k_ref, v_ref, att, act, range_ref, member, spread = buffers
    weight_block, last = weight_copies(weights, buffers, sems)

    start_block(weights, buffers, sems, 1)
    mean, rstd = group_stats(x_ref, member, spread)
    normed[...] = ((x_ref[...] - mean) * rstd).astype(BF16)
    range_ref[0] = jnp.full((8, 128), 1.0, F32)
    range_ref[1] = jnp.full((8, 128), 1.0, F32)

    def heads(j, carry):
        @pl.when(j < BLOCKS - 2)
        def _():
            start_block(weights, buffers, sems, j + 2)

        @pl.when(j == BLOCKS - 2)
        def _():
            last[0].start()

        @pl.when(j == BLOCKS - 1)
        def _():
            last[1].start()

        for i in range(3):
            weight_block(i, j).wait()
        n = normed[...]
        q_ref[j] = (dot(n, wq_s[j]) * (1.0 / 8.0)).astype(BF16)
        k_ref[j] = dot(n, wk_s[j]).astype(BF16)
        v_ref[j] = dot(n, wv_s[j]).astype(BF16)
        lane = lax.broadcasted_iota(jnp.int32, (cells, 128), 1)
        low, high = range_ref[0], range_ref[1]
        for pair in range(2):
            lanes = slice(pair * 128, pair * 128 + 128)
            query = q_ref[j, :, lanes]
            key = k_ref[j, :, lanes]
            value = jnp.concatenate([v_ref[j, :, lanes], jnp.ones((cells, 128), BF16)], axis=1)
            done = []
            for half in range(2):
                mine = jnp.where((lane < HEAD) == (half == 0), query, jnp.zeros_like(query))
                scores = lax.dot_general(
                    mine, key, (((1,), (1,)), ((), ())), preferred_element_type=F32
                )
                out = dot(jnp.exp(scores).astype(BF16), value)
                total = out[:, 128:]
                low = jnp.minimum(low, jnp.min(total.reshape(cells // 8, 8, 128), axis=0))
                high = jnp.maximum(high, jnp.max(total.reshape(cells // 8, 8, 128), axis=0))
                done.append(out[:, :128] / total)
            att[:, pl.ds(pl.multiple_of(j * LANES + pair * 128, 128), 128)] = jnp.where(
                lane < HEAD, done[0], done[1]
            ).astype(BF16)
        range_ref[0] = low
        range_ref[1] = high
        return carry

    lax.fori_loop(0, BLOCKS, heads, 0)
    in_range = jnp.logical_and(jnp.min(range_ref[0]) > LOW_SUM, jnp.max(range_ref[1]) < HIGH_SUM)

    @pl.when(jnp.logical_not(in_range))
    def _():
        def again(j, carry):
            lane = lax.broadcasted_iota(jnp.int32, (cells, 128), 1)
            for pair in range(2):
                done = [safe_head(j, pair, half, q_ref, k_ref, v_ref) for half in range(2)]
                att[:, pl.ds(pl.multiple_of(j * LANES + pair * 128, 128), 128)] = jnp.where(
                    lane < HEAD, done[0], done[1]
                ).astype(BF16)
            return carry

        lax.fori_loop(0, BLOCKS, again, 0)

    last[0].wait()
    for j in range(BLOCKS):
        block = slice(j * LANES, j * LANES + LANES)
        x_ref[:, block] += dot(att[...], wo_s[:, block])

    mean, rstd = group_stats(x_ref, member, spread)
    second = (rows + 2) * TW
    for start, width in ((0, TW), (second, 8)) if side else ((0, TW),):
        act[pl.ds(start, width), :] = jnp.zeros((width, D), F32)
        act[pl.ds(start + (rows + 1) * width, width), :] = jnp.zeros((width, D), F32)
    half_rstd = 0.5 * rstd
    parts = ((0, 0, TW), (middle, second, 8)) if side else ((0, 0, TW),)

    def activate(i, carry):
        for start, place, width in parts:
            size = 4 * width
            at = pl.ds(pl.multiple_of(start + i * size, size), size)
            half = (x_ref[at, :] - mean) * half_rstd
            to = pl.ds(pl.multiple_of(place + width + i * size, 8), size)
            act[to, :] = half + half * jnp.tanh(half)
        return carry

    lax.fori_loop(0, rows // 4, activate, 0)

    def convolve(i, carry):
        spot = lax.broadcasted_iota(jnp.int32, (4, 8, 128), 1)
        for t in range(D // 128):
            lanes = slice(t * 128, t * 128 + 128)
            weight = [taps[n : n + 1, lanes] for n in range(9)]
            sums = [[], [], []]
            for start, place, width in parts:
                size = 4 * width
                lines = [
                    act[pl.ds(pl.multiple_of(place + i * size + d * width, 8), size), lanes]
                    for d in range(3)
                ]
                for dj in range(3):
                    part = lines[0] * weight[dj] + lines[1] * weight[3 + dj] + lines[2] * weight[6 + dj]
                    part = part.reshape(4, width // 8, 8, 128)
                    sums[dj] += [part[:, n] for n in range(width // 8)]
            left = [pltpu.roll(v, 1, 1) for v in sums[0]]
            right = [pltpu.roll(v, 7, 1) for v in sums[2]]
            count = len(left)
            mixed = []
            for n in range(count):
                before = left[n - 1] if side or n > 0 else jnp.zeros_like(left[n])
                after = right[(n + 1) % count] if side or n < count - 1 else jnp.zeros_like(left[n])
                from_left = jnp.where(spot == 0, before, left[n])
                from_right = jnp.where(spot == 7, after, right[n])
                if n == 2:
                    from_left = jnp.where(spot == M, 0.0, from_left)
                    from_right = jnp.where(spot == M - 1, 0.0, from_right)
                mixed.append(sums[1][n] + from_left + from_right)
            centre = jnp.concatenate([mixed[0][:, None], mixed[1][:, None]], axis=1).reshape(4 * TW, 128)
            normed[pl.ds(pl.multiple_of(i * 4 * TW, 4 * TW), 4 * TW), lanes] = centre.astype(BF16)
            if side:
                normed[pl.ds(pl.multiple_of(middle + i * 32, 32), 32), lanes] = (
                    mixed[2].reshape(32, 128).astype(BF16)
                )
        return carry

    lax.fori_loop(0, rows // 4, convolve, 0)
    last[1].wait()
    for j in range(BLOCKS):
        block = slice(j * LANES, j * LANES + LANES)
        emit(block, x_ref[:, block] + dot(normed[...], wp_s[:, block]))


def halves(value):
    return jnp.concatenate([value[:, : D // 2], value[:, D // 2 :]], axis=0)


def tile_kernel(
    above, own, below, left, right, sides, mains, strips, wq, wk, wv, wo, taps, wp,
    main, to_left, to_right, centre, rims, x_ref, out, out_side, part_sems, sems, *buffers,
):
    copies, start = [], 0
    for i, piece in enumerate((above, own, below)):
        size = piece.shape[0]
        copies.append(pltpu.make_async_copy(piece, centre.at[pl.ds(start, size)], part_sems.at[i]))
        start += size
    copies.append(pltpu.make_async_copy(left, rims.at[pl.ds(0, STRIP)], part_sems.at[3]))
    copies.append(pltpu.make_async_copy(right, rims.at[pl.ds(STRIP, STRIP)], part_sems.at[4]))
    for copy in copies:
        copy.start()
    weights = (wq, wk, wv, wo, taps, wp)
    start_block(weights, buffers, sems, 0)
    group_matrices(buffers[-2], buffers[-1])
    for copy in copies:
        copy.wait()
    x_ref[pl.ds(0, SENT), :] = centre[...].astype(F32)
    x_ref[pl.ds(SENT, SIDE), :] = dot(sides[...], rims[...])

    def emit(block, values):
        rounded = values.astype(BF16)
        out[:, block] = rounded[:SENT]
        out_side[:, block] = rounded[SENT:].astype(F32)

    refine(WH, True, x_ref, weights, buffers, sems, emit)
    for a in range(N_ROW):
        first = (a + M) % N_ROW
        lines = [out[(8 * k + first) * TW : (8 * k + first + 1) * TW, :] for k in range(4)]
        main[a * 128 : a * 128 + 128, :] = dot(
            mains[...], halves(jnp.concatenate(lines, axis=0))
        ).astype(BF16)
        lines = [out_side[(8 * k + first) * 8 : (8 * k + first + 1) * 8, :] for k in range(4)]
        rim = dot(strips[...], halves(jnp.concatenate(lines, axis=0).astype(BF16))).astype(BF16)
        to_right[a * 32 : a * 32 + 32, :] = rim[:32]
        to_left[a * 32 : a * 32 + 32, :] = rim[32:]


def join_kernel(main, from_left, from_right, out):
    for a in range(N_ROW):
        first, last = a * 128, a * 128 + 96
        rim = slice(a * 32, a * 32 + 32)
        out[first : first + 32, :] = (
            main[first : first + 32, :].astype(F32) + from_left[rim, :].astype(F32)
        ).astype(BF16)
        out[first + 32 : last, :] = main[first + 32 : last, :]
        out[last : last + 32, :] = (
            main[last : last + 32, :].astype(F32) + from_right[rim, :].astype(F32)
        ).astype(BF16)


def sub_kernel(
    place, got, gathers, packing, wq, wk, wv, wo, taps, wp,
    result, gather, local, x_ref, out, gather_sem, sems, *buffers,
):
    weights = (wq, wk, wv, wo, taps, wp)
    copy = pltpu.make_async_copy(gathers.at[place[0]], gather, gather_sem)
    copy.start()
    start_block(weights, buffers, sems, 0)
    group_matrices(buffers[-2], buffers[-1])
    late = place[1]
    copy.wait()
    for r in range(N_ROW):
        other = jnp.clip(r + 2 * late - 1, 0, N_ROW - 1)
        edge = 1 - late if r == 0 else late if r == N_ROW - 1 else 0
        cells = jnp.concatenate(
            [got[r * 128 : r * 128 + 128, :], got[pl.ds(pl.multiple_of(other * 128, 128), 128), :]],
            axis=0,
        )
        value = dot(gather[edge], cells).astype(BF16)
        at = slice(r * 48, r * 48 + 48)
        for h in range(2):
            half = slice(h * D // 2, h * D // 2 + D // 2)
            local[at, half] = value[h * 48 : h * 48 + 48]
            x_ref[at, half] = value[h * 48 : h * 48 + 48].astype(F32)

    def emit(block, values):
        dilated = values.astype(BF16).astype(F32)
        out[:, block] = (0.6 * local[:, block].astype(F32) + 0.4 * dilated).astype(BF16)

    refine(TH, False, x_ref, weights, buffers, sems, emit)
    for r in range(N_ROW):
        at = slice(r * 48, r * 48 + 48)
        cells = jnp.concatenate([out[at, t * LANES : t * LANES + LANES] for t in range(BLOCKS)], axis=0)
        packed = dot(packing[...], cells).astype(BF16)
        result[r * 128 : r * 128 + 128, :LANES] = packed[:128]
        result[r * 128 : r * 128 + 128, LANES:] = packed[128:]


def unpack_kernel(got, packing, out):
    for a in range(N_ROW):
        at = slice(a * 128, a * 128 + 128)
        cells = jnp.concatenate([got[at, :LANES], got[at, LANES:]], axis=0)
        value = lax.dot_general(
            packing[...], cells, (((0,), (0,)), ((), ())), preferred_element_type=F32
        ).astype(BF16)
        for t in range(BLOCKS):
            for i in range(PART_H):
                to = (i * N_ROW + a) * TW
                out[to : to + TW, t * LANES : t * LANES + LANES] = value[
                    t * 48 + i * TW : t * 48 + i * TW + TW
                ]


def scratch(cells, padded):
    heads = pltpu.VMEM((BLOCKS, cells, LANES), BF16)
    blocks = pltpu.VMEM((BLOCKS, D, LANES), BF16)
    square = pltpu.VMEM((D, D), BF16)
    return [
        pltpu.SemaphoreType.DMA((5, BLOCKS)),
        blocks, blocks, blocks, square, square,
        pltpu.VMEM((cells, D), BF16),
        heads, heads, heads,
        pltpu.VMEM((cells, D), BF16),
        pltpu.VMEM((padded, D), F32),
        pltpu.VMEM((2, 8, 128), F32),
        pltpu.VMEM((D, 128), BF16),
        pltpu.VMEM((128, D), BF16),
    ]


ANY = pl.BlockSpec(memory_space=pl.ANY)
VMEM = pl.BlockSpec(memory_space=pltpu.VMEM)
PARAMS = dict(vmem_limit_bytes=56 * 2**20)


def tile_block(above, own, below, left, right, weights):
    shape = jax.ShapeDtypeStruct
    return pl.pallas_call(
        tile_kernel,
        out_shape=(
            shape((2 * SENT, D // 2), BF16),
            shape((2 * STRIP, D // 2), BF16),
            shape((2 * STRIP, D // 2), BF16),
        ),
        in_specs=[ANY] * 5 + [VMEM] * 3 + [ANY] * 4 + [VMEM, ANY],
        out_specs=(VMEM, VMEM, VMEM),
        scratch_shapes=[
            pltpu.VMEM((SENT, D), BF16),
            pltpu.VMEM((SIDE, D), BF16),
            pltpu.VMEM((WIN, D), F32),
            pltpu.VMEM((SENT, D), BF16),
            pltpu.VMEM((SIDE, D), F32),
            pltpu.SemaphoreType.DMA((5,)),
            *scratch(WIN, (WH + 2) * WW),
        ],
        compiler_params=pltpu.CompilerParams(**PARAMS),
        name="tile_block",
    )(above, own, below, left, right, side_matrix(), main_matrix(), strip_matrix(), *weights)


def join(main, from_left, from_right):
    return pl.pallas_call(
        join_kernel,
        out_shape=jax.ShapeDtypeStruct(main.shape, BF16),
        in_specs=[VMEM] * 3,
        out_specs=VMEM,
        name="join",
    )(main, from_left, from_right)


def sub_block(place, got, weights):
    return pl.pallas_call(
        sub_kernel,
        out_shape=jax.ShapeDtypeStruct((DEV * 8, 2 * LANES), BF16),
        in_specs=[pl.BlockSpec(memory_space=pltpu.SMEM), VMEM, ANY, VMEM] + [ANY] * 4 + [VMEM, ANY],
        out_specs=VMEM,
        scratch_shapes=[
            pltpu.VMEM((2, 96, 256), BF16),
            pltpu.VMEM((OWN, D), BF16),
            pltpu.VMEM((OWN, D), F32),
            pltpu.VMEM((OWN, D), BF16),
            pltpu.SemaphoreType.DMA,
            *scratch(OWN, (TH + 2) * TW),
        ],
        compiler_params=pltpu.CompilerParams(**PARAMS),
        name="sub_block",
    )(place, got, gather_matrices(), packing_matrix(), *weights)


def unpack(got):
    return pl.pallas_call(
        unpack_kernel,
        out_shape=jax.ShapeDtypeStruct((OWN, D), BF16),
        in_specs=[VMEM] * 2,
        out_specs=VMEM,
        name="unpack",
    )(got, packing_matrix())


def shift(value, axis, step):
    count = lax.axis_size(axis)
    pairs = [(i, i + step) for i in range(count) if 0 <= i + step < count]
    return lax.ppermute(value, axis, pairs)


def body(latent, w_query, w_key, w_value, w_out, depth_kernel, w_proj):
    weights = (w_query, w_key, w_value, w_out, depth_kernel, w_proj)
    row, col = lax.axis_index("row"), lax.axis_index("col")
    late = (row >= M).astype(jnp.int32)
    kind = (col >= M).astype(jnp.int32) + (col >= TW - M).astype(jnp.int32)
    place = jnp.stack([3 * late + kind, late])
    above = shift(latent[TH - M :], "row", 1)
    below = shift(latent[:M], "row", -1)
    tall = jnp.concatenate([above, latent, below], axis=0)
    left = shift(tall[:, TW - M :].reshape(STRIP, D), "col", 1)
    right = shift(tall[:, :M].reshape(STRIP, D), "col", -1)
    main, to_left, to_right = tile_block(
        above.reshape(M * TW, D), latent.reshape(OWN, D), below.reshape(M * TW, D),
        left, right, weights,
    )
    main = join(main, shift(to_right, "col", 1), shift(to_left, "col", -1))
    both = functools.partial(
        lax.all_to_all, axis_name=("row", "col"), split_axis=0, concat_axis=0, tiled=True
    )
    got = both(main.reshape(DEV, 8, D // 2)).reshape(2 * SENT, D // 2)
    refined = sub_block(place, got, weights)
    back = both(refined.reshape(DEV, 8, 2 * LANES)).reshape(DEV * 8, 2 * LANES)
    return unpack(back).reshape(TH, TW, D)


def solution(mesh):
    return jax.shard_map(
        body,
        mesh=mesh,
        in_specs=(P("row", "col", None), P(), P(), P(), P(), P(), P()),
        out_specs=P("row", "col", None),
        check_vma=False,
    )
```

time: 179 us -> 171 us (0.955)
  other arithmetic: 7.44 us -> 0.61 us
  local copies, waits for them, and re-layouts: 10.3 us -> 4.16 us
  waiting for transfers between devices: 36.6 us -> 42.6 us
    ppermute x6, waiting for transfers between devices: 16.6 us -> 21.2 us  [shift(): return lax.ppermute(value, axis, pairs)]
    reshape x3 -> x0, local copies, waits for them, and re-layouts: 3.98 us -> none  [the longest x2 2.76 us: body(): back = both(refined.reshape(DEV, 30, 128)).reshape(N_ROW, N_COL, PART_H, D)]
    convert_element_type x2 -> x0, other arithmetic: 3.71 us -> none  [the longest x1 1.88 us: body(): main = main.reshape(N_ROW, TW, 4, D).astype(F32)]
    convert_element_type x3 -> x0, local copies, waits for them, and re-layouts: 2.92 us -> none  [the longest x1 2.61 us: body(): main = main.reshape(N_ROW, TW, 4, D).astype(F32)]
    concatenate x1 -> x0, other arithmetic: 1.99 us -> none  [body(): jnp.concatenate([main[:, :M] + from_left, main[:, M:TW - M], main[:, TW -...]
    unnamed x14 -> x18, local copies, waits for them, and re-layouts: 0.84 us -> 2.63 us
    pallas_call x2 -> x4, Pallas kernels: 71.2 us -> 69.9 us  [the longest x1 41 us: tile_block(): pl.pallas_call(tile_kernel, out_shape=(shape((2 * SENT, D // 2), BF16), s...]
  transfers between devices with their start and end apart: 7 -> 7, of which waited for: 6 -> 7; matrix products, arithmetic and copies ran while one was open for 4% -> 0% of each run, Pallas kernels for 0% -> 0%
where the time goes in v1:
time: 171 us
  Pallas kernels  69.9 us (41%)
  waiting for transfers between devices  42.6 us (25%)
  starting transfers between devices  29.5 us (17%)
  blocking collectives  23.8 us (14%)
  local copies, waits for them, and re-layouts  4.16 us (2%)
    pallas_call x1, Pallas kernels, tile_block(): pl.pallas_call(tile_kernel, out_shape=(shape((2 * SENT, D // 2), BF16), s...  41 us
    all_to_all x1, blocking collectives, body(): back = both(refined.reshape(DEV, 8, 2 * LANES)).reshape(DEV * 8, 2 * LANES)  23.8 us
    pallas_call x1, Pallas kernels, sub_block(): pl.pallas_call(sub_kernel, out_shape=jax.ShapeDtypeStruct((DEV * 8, 2 * L...  23.6 us
    all_to_all x1, waiting for transfers between devices, body(): got = both(main.reshape(DEV, 8, D // 2)).reshape(2 * SENT, D // 2)  21.3 us
    ppermute x6, waiting for transfers between devices, shift(): return lax.ppermute(value, axis, pairs)  21.2 us
    ppermute x6, starting transfers between devices, shift(): return lax.ppermute(value, axis, pairs)  18.1 us
    all_to_all x1, starting transfers between devices, body(): got = both(main.reshape(DEV, 8, D // 2)).reshape(2 * SENT, D // 2)  11.4 us
  transfers between devices with their start and end apart: 7, of which 7 were waited for; matrix products, arithmetic and copies ran while one was open for 0% of the time, Pallas kernels for 0%

profile of v1, /device:TPU:1, one launch (start us, length us, event | category | flops | bytes accessed | tf_op | source)
XLA Modules:
  0.0 170.7 jit_solution(9846989251459059451)
XLA Ops:
  0.0 1.1 fusion.1
  1.1 4.0 %collective-permute-start = (bf16[4,16,1280]{2,1,0:T(8,128)(2,1)S(1)}, bf16[4,16,1280]{2,1,0:T(8,128)(2,1)S(1)}, u32[]{:S(2)}, u32[]{:S(2)}) collective-permute-start(bf16[4,16,1280]{2,1,0:T(8,128)(2,1)S(1)} %get-tuple-element.14), channel_id=1, source_target_pairs={{0,16},{16,32},{32,48},{48,64},{64,80},{80,96},{96,112},{1,17},{17... | collective-permute-start | bytes 491528 | tf_op jit(solution)/shard_map/ppermute | solution.py:503
  5.1 1.3 collective-permute-start.1
  6.4 1.5 collective-permute-done
  8.0 3.7 %collective-permute-done.1 = bf16[4,16,1280]{2,1,0:T(8,128)(2,1)S(1)} collective-permute-done((bf16[4,16,1280]{2,1,0:T(8,128)(2,1)S(1)}, bf16[4,16,1280]{2,1,0:T(8,128)(2,1)S(1)}, u32[]{:S(2)}, u32[]{:S(2)}) %collective-permute-start.1) | collective-permute-done | bytes 163872 | tf_op jit(solution)/shard_map/ppermute | solution.py:503
  12.1 6.6 %collective-permute-start.2 = (bf16[128,1280]{1,0:T(8,128)(2,1)S(1)}, bf16[128,1280]{1,0:T(8,128)(2,1)S(1)}, u32[]{:S(2)}, u32[]{:S(2)}) collective-permute-start(bf16[128,1280]{1,0:T(8,128)(2,1)S(1)} %reshape.33), channel_id=1, source_target_pairs={{0,1},{1,2},{2,3},{3,4},{4,5},{5,6},{6,7},{7,8},{8,9},{9,10},{10,1... | collective-permute-start | bytes 983048 | tf_op jit(solution)/shard_map/ppermute | solution.py:503
  18.8 1.9 %collective-permute-start.3 = (bf16[128,1280]{1,0:T(8,128)(2,1)S(1)}, bf16[128,1280]{1,0:T(8,128)(2,1)S(1)}, u32[]{:S(2)}, u32[]{:S(2)}) collective-permute-start(bf16[128,1280]{1,0:T(8,128)(2,1)S(1)} %reshape.34), channel_id=1, source_target_pairs={{1,0},{2,1},{3,2},{4,3},{5,4},{6,5},{7,6},{8,7},{9,8},{10,9},{11,1... | collective-permute-start | bytes 983048 | tf_op jit(solution)/shard_map/ppermute | solution.py:503
  20.7 2.0 %collective-permute-done.2.left = bf16[128,1280]{1,0:T(8,128)(2,1)S(1)} collective-permute-done((bf16[128,1280]{1,0:T(8,128)(2,1)S(1)}, bf16[128,1280]{1,0:T(8,128)(2,1)S(1)}, u32[]{:S(2)}, u32[]{:S(2)}) %collective-permute-start.2) | collective-permute-done | bytes 327712 | tf_op jit(solution)/shard_map/ppermute | solution.py:503
  22.7 6.0 %collective-permute-done.3.right = bf16[128,1280]{1,0:T(8,128)(2,1)S(1)} collective-permute-done((bf16[128,1280]{1,0:T(8,128)(2,1)S(1)}, bf16[128,1280]{1,0:T(8,128)(2,1)S(1)}, u32[]{:S(2)}, u32[]{:S(2)}) %collective-permute-start.3) | collective-permute-done | bytes 327712 | tf_op jit(solution)/shard_map/ppermute | solution.py:503
  28.7 0.7 copy-done.7
  29.4 41.0 %tile_block.1 = (bf16[1024,640]{1,0:T(8,128)(2,1)}, bf16[256,640]{1,0:T(8,128)(2,1)}, bf16[256,640]{1,0:T(8,128)(2,1)}) custom-call(bf16[64,1280]{1,0:T(8,128)(2,1)} %bitcast.15, bf16[384,1280]{1,0:T(8,128)(2,1)} %bitcast.10, bf16[64,1280]{1,0:T(8,128)(2,1)} %bitcast.16, bf16[128,1280]{1,0:T(8,128)(2,1)} %copy-done.6, bf16[128,1280]{1,0:T(8,128)(2,1)} %copy-done.7, ...), custom_call_target="tpu_custom_call" | custom-call | tf_op jit(solution)/shard_map/tile_block/pallas_call | solution.py:438
  70.3 1.9 %collective-permute-start.4 = (bf16[256,640]{1,0:T(8,128)(2,1)}, bf16[256,640]{1,0:T(8,128)(2,1)S(1)}, u32[]{:S(2)}, u32[]{:S(2)}) collective-permute-start(bf16[256,640]{1,0:T(8,128)(2,1)} %get-tuple-element.9), channel_id=1, source_target_pairs={{0,1},{1,2},{2,3},{3,4},{4,5},{5,6},{6,7},{7,8},{8,9},{9,10},{10,1... | collective-permute-start | bytes 983048 | tf_op jit(solution)/shard_map/ppermute | solution.py:503
  72.3 2.4 %collective-permute-start.5 = (bf16[256,640]{1,0:T(8,128)(2,1)}, bf16[256,640]{1,0:T(8,128)(2,1)S(1)}, u32[]{:S(2)}, u32[]{:S(2)}) collective-permute-start(bf16[256,640]{1,0:T(8,128)(2,1)} %get-tuple-element.10), channel_id=1, source_target_pairs={{1,0},{2,1},{3,2},{4,3},{5,4},{6,5},{7,6},{8,7},{9,8},{10,9},{11,1... | collective-permute-start | bytes 983048 | tf_op jit(solution)/shard_map/ppermute | solution.py:503
  74.7 1.9 %collective-permute-done.4.from_left = bf16[256,640]{1,0:T(8,128)(2,1)S(1)} collective-permute-done((bf16[256,640]{1,0:T(8,128)(2,1)}, bf16[256,640]{1,0:T(8,128)(2,1)S(1)}, u32[]{:S(2)}, u32[]{:S(2)}) %collective-permute-start.4) | collective-permute-done | bytes 327712 | tf_op jit(solution)/shard_map/ppermute | solution.py:503
  76.6 6.2 %collective-permute-done.5.from_right = bf16[256,640]{1,0:T(8,128)(2,1)S(1)} collective-permute-done((bf16[256,640]{1,0:T(8,128)(2,1)}, bf16[256,640]{1,0:T(8,128)(2,1)S(1)}, u32[]{:S(2)}, u32[]{:S(2)}) %collective-permute-start.5) | collective-permute-done | bytes 327712 | tf_op jit(solution)/shard_map/ppermute | solution.py:503
  82.7 0.7 copy-done.5
  83.5 2.7 %join.1 = bf16[1024,640]{1,0:T(8,128)(2,1)} custom-call(bf16[1024,640]{1,0:T(8,128)(2,1)} %get-tuple-element.8.main, bf16[256,640]{1,0:T(8,128)(2,1)} %copy-done.4, bf16[256,640]{1,0:T(8,128)(2,1)} %copy-done.5), custom_call_target="tpu_custom_call" | custom-call | tf_op jit(solution)/shard_map/join/pallas_call | solution.py:462
  86.2 11.4 %all-to-all-start = ((bf16[128,8,640]{2,1,0:T(8,128)(2,1)}), bf16[128,8,640]{2,1,0:T(8,128)(2,1)S(1)}, u32[]{:S(2)}, u32[]{:S(2)}) async-start(bf16[128,8,640]{2,1,0:T(8,128)(2,1)} %bitcast.12), calls=%async_computation | async-start | bytes 2621440 | tf_op jit(solution)/shard_map/all_to_all | solution.py:525
  97.6 0.6 pad_add_fusion.place
  98.2 21.3 %all-to-all-done = bf16[128,8,640]{2,1,0:T(8,128)(2,1)S(1)} async-done(((bf16[128,8,640]{2,1,0:T(8,128)(2,1)}), bf16[128,8,640]{2,1,0:T(8,128)(2,1)S(1)}, u32[]{:S(2)}, u32[]{:S(2)}) %all-to-all-start) | async-done | bytes 1310752 | tf_op jit(solution)/shard_map/all_to_all | solution.py:525
  119.6 1.1 copy-done.1
  120.6 23.6 %sub_block.1 = bf16[1024,512]{1,0:T(8,128)(2,1)} custom-call(s32[2]{0:T(128)} %pad_add_fusion.place, bf16[1024,640]{1,0:T(8,128)(2,1)} %bitcast.11, bf16[6,2,96,256]{3,2,1,0:T(8,128)(2,1)} %constant.30.clone.gathers, bf16[256,240]{1,0:T(8,128)(2,1)} %constant.31.clone.packing, bf16[1280,1280]{1,0:T(8,128)(2,1)} %wq.3, bf16[1280,1280]{1,0:T(8,128)(2,1)} %wk.3, ...), custom_call_target="tpu_custom_call" | custom-call | tf_op jit(solution)/shard_map/sub_block/pallas_call | solution.py:472
  144.3 23.8 %all_to_all.10 = bf16[128,8,512]{2,1,0:T(8,128)(2,1)} all-to-all(bf16[128,8,512]{2,1,0:T(8,128)(2,1)} %bitcast.13), channel_id=1, replica_groups=mesh['row'=8,'col'=16] {'row','col'}, dimensions={0} | all-to-all | bytes 2097152 | tf_op jit(solution)/shard_map/all_to_all | solution.py:527
  168.1 2.7 %unpack.1 = bf16[384,1280]{1,0:T(8,128)(2,1)} custom-call(bf16[1024,512]{1,0:T(8,128)(2,1)} %bitcast.14, bf16[256,240]{1,0:T(8,128)(2,1)} %constant.31.clone.packing), custom_call_target="tpu_custom_call" | custom-call | tf_op jit(solution)/shard_map/unpack/pallas_call | solution.py:491
  (19 shorter events, 0.5 us)
Async XLA Ops:
  0.0 7.9 %copy-start = (bf16[24,16,1280]{2,1,0:T(8,128)(2,1)S(1)}, bf16[24,16,1280]{2,1,0:T(8,128)(2,1)}, u32[]{:S(2)}) copy-start(bf16[24,16,1280]{2,1,0:T(8,128)(2,1)} %param.13) | copy-start | bytes 2949124
  1.1 6.8 %collective-permute-start = (bf16[4,16,1280]{2,1,0:T(8,128)(2,1)S(1)}, bf16[4,16,1280]{2,1,0:T(8,128)(2,1)S(1)}, u32[]{:S(2)}, u32[]{:S(2)}) collective-permute-start(bf16[4,16,1280]{2,1,0:T(8,128)(2,1)S(1)} %get-tuple-element.14), channel_id=1, source_target_pairs={{0,16},{16,32},{32,48},{48,64},{64,80},{80,96},{96,112},{1,17},{17... | collective-permute-start | bytes 491528 | tf_op jit(solution)/shard_map/ppermute | solution.py:503
  5.1 6.6 %collective-permute-start.1 = (bf16[4,16,1280]{2,1,0:T(8,128)(2,1)S(1)}, bf16[4,16,1280]{2,1,0:T(8,128)(2,1)S(1)}, u32[]{:S(2)}, u32[]{:S(2)}) collective-permute-start(bf16[4,16,1280]{2,1,0:T(8,128)(2,1)S(1)} %get-tuple-element.13), channel_id=1, source_target_pairs={{16,0},{32,16},{48,32},{64,48},{80,64},{96,80},{112,96},{17,1},{33... | collective-permute-start | bytes 491528 | tf_op jit(solution)/shard_map/ppermute | solution.py:503
  7.9 4.1 %copy-start.2 = (bf16[4,16,1280]{2,1,0:T(8,128)(2,1)}, bf16[4,16,1280]{2,1,0:T(8,128)(2,1)S(1)}, u32[]{:S(2)}) copy-start(bf16[4,16,1280]{2,1,0:T(8,128)(2,1)S(1)} %collective-permute-done) | copy-start | bytes 491524
  11.7 7.0 %copy-start.3 = (bf16[4,16,1280]{2,1,0:T(8,128)(2,1)}, bf16[4,16,1280]{2,1,0:T(8,128)(2,1)S(1)}, u32[]{:S(2)}) copy-start(bf16[4,16,1280]{2,1,0:T(8,128)(2,1)S(1)} %collective-permute-done.1) | copy-start | bytes 491524
  12.1 10.6 %collective-permute-start.2 = (bf16[128,1280]{1,0:T(8,128)(2,1)S(1)}, bf16[128,1280]{1,0:T(8,128)(2,1)S(1)}, u32[]{:S(2)}, u32[]{:S(2)}) collective-permute-start(bf16[128,1280]{1,0:T(8,128)(2,1)S(1)} %reshape.33), channel_id=1, source_target_pairs={{0,1},{1,2},{2,3},{3,4},{4,5},{5,6},{6,7},{7,8},{8,9},{9,10},{10,1... | collective-permute-start | bytes 983048 | tf_op jit(solution)/shard_map/ppermute | solution.py:503
  18.8 9.9 %collective-permute-start.3 = (bf16[128,1280]{1,0:T(8,128)(2,1)S(1)}, bf16[128,1280]{1,0:T(8,128)(2,1)S(1)}, u32[]{:S(2)}, u32[]{:S(2)}) collective-permute-start(bf16[128,1280]{1,0:T(8,128)(2,1)S(1)} %reshape.34), channel_id=1, source_target_pairs={{1,0},{2,1},{3,2},{4,3},{5,4},{6,5},{7,6},{8,7},{9,8},{10,9},{11,1... | collective-permute-start | bytes 983048 | tf_op jit(solution)/shard_map/ppermute | solution.py:503
  22.7 6.0 %copy-start.6 = (bf16[128,1280]{1,0:T(8,128)(2,1)}, bf16[128,1280]{1,0:T(8,128)(2,1)S(1)}, u32[]{:S(2)}) copy-start(bf16[128,1280]{1,0:T(8,128)(2,1)S(1)} %collective-permute-done.2.left) | copy-start | bytes 983044
  28.7 0.7 copy-start.7
  70.3 6.2 %collective-permute-start.4 = (bf16[256,640]{1,0:T(8,128)(2,1)}, bf16[256,640]{1,0:T(8,128)(2,1)S(1)}, u32[]{:S(2)}, u32[]{:S(2)}) collective-permute-start(bf16[256,640]{1,0:T(8,128)(2,1)} %get-tuple-element.9), channel_id=1, source_target_pairs={{0,1},{1,2},{2,3},{3,4},{4,5},{5,6},{6,7},{7,8},{8,9},{9,10},{10,1... | collective-permute-start | bytes 983048 | tf_op jit(solution)/shard_map/ppermute | solution.py:503
  72.3 10.5 %collective-permute-start.5 = (bf16[256,640]{1,0:T(8,128)(2,1)}, bf16[256,640]{1,0:T(8,128)(2,1)S(1)}, u32[]{:S(2)}, u32[]{:S(2)}) collective-permute-start(bf16[256,640]{1,0:T(8,128)(2,1)} %get-tuple-element.10), channel_id=1, source_target_pairs={{1,0},{2,1},{3,2},{4,3},{5,4},{6,5},{7,6},{8,7},{9,8},{10,9},{11,1... | collective-permute-start | bytes 983048 | tf_op jit(solution)/shard_map/ppermute | solution.py:503
  76.6 6.2 %copy-start.4 = (bf16[256,640]{1,0:T(8,128)(2,1)}, bf16[256,640]{1,0:T(8,128)(2,1)S(1)}, u32[]{:S(2)}) copy-start(bf16[256,640]{1,0:T(8,128)(2,1)S(1)} %collective-permute-done.4.from_left) | copy-start | bytes 983044
  82.7 0.7 copy-start.5
  86.2 33.4 %all-to-all-start = ((bf16[128,8,640]{2,1,0:T(8,128)(2,1)}), bf16[128,8,640]{2,1,0:T(8,128)(2,1)S(1)}, u32[]{:S(2)}, u32[]{:S(2)}) async-start(bf16[128,8,640]{2,1,0:T(8,128)(2,1)} %bitcast.12), calls=%async_computation | async-start | bytes 2621440 | tf_op jit(solution)/shard_map/all_to_all | solution.py:525
  119.6 1.1 copy-start.1

commit v2 on v1

--- a/solution.py
+++ b/solution.py
@@ -33,6 +33,8 @@
 BF16 = jnp.bfloat16
 HIGH_SUM = 2.0**100
 LOW_SUM = 2.0**-100
+TILE_MIB = 48
+REST_MIB = 14
 
 
 def side_matrix():
@@ -95,15 +97,21 @@
     return jnp.dot(a, b, preferred_element_type=F32)
 
 
-def three_parts(row):
-    full = jnp.broadcast_to(row, (8, row.shape[1]))
+def six_parts(first, second):
+    shape = (8, first.shape[1])
+    which = lax.broadcasted_iota(jnp.int32, shape, 0)
+    full = jnp.where(which < 3, jnp.broadcast_to(first, shape), jnp.broadcast_to(second, shape))
     high = full.astype(BF16).astype(F32)
     rest = full - high
     mid = rest.astype(BF16).astype(F32)
     low = rest - mid
-    which = lax.broadcasted_iota(jnp.int32, full.shape, 0)
-    parts = jnp.where(which == 0, high, jnp.where(which == 1, mid, jnp.where(which == 2, low, 0.0)))
-    return parts.astype(BF16)
+    part = jnp.where(which < 3, which, which - 3)
+    parts = jnp.where(part == 0, high, jnp.where(part == 1, mid, low))
+    return jnp.where(which < 6, parts, 0.0).astype(BF16)
+
+
+def two_rows(parts):
+    return parts[0:1] + parts[1:2] + parts[2:3], parts[3:4] + parts[4:5] + parts[5:6]
 
 
 def group_matrices(member, spread):
@@ -114,16 +122,37 @@
         ref[...] = jnp.where(inside, 1.0, 0.0).astype(BF16)
 
 
-def group_mean(row, count, member, spread):
-    sums = jnp.sum(dot(three_parts(row), member[...]), axis=0, keepdims=True) * (1.0 / (GROUP * count))
-    return jnp.sum(dot(three_parts(sums), spread[...]), axis=0, keepdims=True)
-
-
-def group_stats(x_ref, member, spread):
-    cells = x_ref.shape[0]
-    mean = group_mean(jnp.sum(x_ref[...], axis=0, keepdims=True), cells, member, spread)
-    var = group_mean(jnp.sum(jnp.square(x_ref[...] - mean), axis=0, keepdims=True), cells, member, spread)
-    return mean, 1.0 / jnp.sqrt(var + 1e-05)
+def add_sums(sums, lanes, value):
+    tiles = value.reshape(value.shape[0] // 8, 8, value.shape[1])
+    sums[0:8, lanes] += jnp.sum(tiles, axis=0)
+    sums[8:16, lanes] += jnp.sum(tiles * tiles, axis=0)
+
+
+def group_stats(x_ref, sums, stats, member, spread):
+    scale = 1.0 / (GROUP * x_ref.shape[0])
+
+    def means(first, second):
+        first, second = two_rows(dot(six_parts(first, second), member[...]))
+        return first * scale, second * scale
+
+    def spread_out(mean, var):
+        rstd = 1.0 / jnp.sqrt(jnp.maximum(var, 0.0) + 1e-05)
+        mean, rstd = two_rows(dot(six_parts(mean, rstd), spread[...]))
+        stats[0:1] = mean
+        stats[1:2] = rstd
+
+    total = jnp.sum(sums[0:8], axis=0, keepdims=True)
+    mean, square = means(total, jnp.sum(sums[8:16], axis=0, keepdims=True))
+    var = square - mean * mean
+    spread_out(mean, var)
+
+    @pl.when(jnp.logical_not(jnp.min(var - 0.01 * mean * mean) >= 0.0))
+    def _():
+        centred = jnp.square(x_ref[...] - stats[0:1])
+        _, var = means(total, jnp.sum(centred, axis=0, keepdims=True))
+        spread_out(mean, var)
+
+    return stats[0:1], stats[1:2]
 
 
 def safe_head(j, pair, half, q_ref, k_ref, v_ref):
@@ -161,15 +190,15 @@
         block(i, j).start()
 
 
-def refine(rows, side, x_ref, weights, buffers, sems, emit):
+def refine(rows, side, x_ref, weights, buffers, sems):
     cells = x_ref.shape[0]
     middle = rows * TW
     taps = weights[4]
-    wq_s, wk_s, wv_s, wo_s, wp_s, normed, q_ref, k_ref, v_ref, att, act, range_ref, member, spread = buffers
+    wq_s, wk_s, wv_s, wo_s, wp_s, normed, q_ref, k_ref, v_ref, att, act, range_ref, member, spread, sums, stats = buffers
     weight_block, last = weight_copies(weights, buffers, sems)
 
     start_block(weights, buffers, sems, 1)
-    mean, rstd = group_stats(x_ref, member, spread)
+    mean, rstd = group_stats(x_ref, sums, stats, member, spread)
     normed[...] = ((x_ref[...] - mean) * rstd).astype(BF16)
     range_ref[0] = jnp.full((8, 128), 1.0, F32)
     range_ref[1] = jnp.full((8, 128), 1.0, F32)
@@ -234,12 +263,15 @@
 
         lax.fori_loop(0, BLOCKS, again, 0)
 
+    sums[...] = jnp.zeros_like(sums)
     last[0].wait()
     for j in range(BLOCKS):
         block = slice(j * LANES, j * LANES + LANES)
-        x_ref[:, block] += dot(att[...], wo_s[:, block])
-
-    mean, rstd = group_stats(x_ref, member, spread)
+        hidden = x_ref[:, block] + dot(att[...], wo_s[:, block])
+        x_ref[:, block] = hidden
+        add_sums(sums, block, hidden)
+
+    mean, rstd = group_stats(x_ref, sums, stats, member, spread)
     second = (rows + 2) * TW
     for start, width in ((0, TW), (second, 8)) if side else ((0, TW),):
         act[pl.ds(start, width), :] = jnp.zeros((width, D), F32)
@@ -297,9 +329,6 @@
 
     lax.fori_loop(0, rows // 4, convolve, 0)
     last[1].wait()
-    for j in range(BLOCKS):
-        block = slice(j * LANES, j * LANES + LANES)
-        emit(block, x_ref[:, block] + dot(normed[...], wp_s[:, block]))
 
 
 def halves(value):
@@ -307,9 +336,10 @@
 
 
 def tile_kernel(
-    above, own, below, left, right, sides, mains, strips, wq, wk, wv, wo, taps, wp,
-    main, to_left, to_right, centre, rims, x_ref, out, out_side, part_sems, sems, *buffers,
+    above, own, below, left, right, sides, strips, wq, wk, wv, wo, taps, wp,
+    to_left, to_right, x_ref, normed, wp_s, centre, rims, out_side, part_sems, sems, *buffers,
 ):
+    buffers = (*buffers[:4], wp_s, normed, *buffers[4:])
     copies, start = [], 0
     for i, piece in enumerate((above, own, below)):
         size = piece.shape[0]
@@ -321,28 +351,43 @@
         copy.start()
     weights = (wq, wk, wv, wo, taps, wp)
     start_block(weights, buffers, sems, 0)
-    group_matrices(buffers[-2], buffers[-1])
+    group_matrices(buffers[-4], buffers[-3])
+    sums = buffers[-2]
+    sums[...] = jnp.zeros_like(sums)
     for copy in copies:
         copy.wait()
-    x_ref[pl.ds(0, SENT), :] = centre[...].astype(F32)
-    x_ref[pl.ds(SENT, SIDE), :] = dot(sides[...], rims[...])
-
-    def emit(block, values):
-        rounded = values.astype(BF16)
-        out[:, block] = rounded[:SENT]
-        out_side[:, block] = rounded[SENT:].astype(F32)
-
-    refine(WH, True, x_ref, weights, buffers, sems, emit)
+    for j in range(BLOCKS):
+        block = slice(j * LANES, j * LANES + LANES)
+        value = centre[:, block].astype(F32)
+        x_ref[:SENT, block] = value
+        add_sums(sums, block, value)
+        value = dot(sides[...], rims[:, block])
+        x_ref[SENT:, block] = value
+        add_sums(sums, block, value)
+
+    refine(WH, True, x_ref, weights, buffers, sems)
+    for j in range(BLOCKS):
+        block = slice(j * LANES, j * LANES + LANES)
+        value = x_ref[SENT:, block] + dot(normed[SENT:, :], wp_s[:, block])
+        out_side[:, block] = value.astype(BF16).astype(F32)
+    for a in range(N_ROW):
+        first = (a + M) % N_ROW
+        lines = [out_side[(8 * k + first) * 8 : (8 * k + first + 1) * 8, :] for k in range(4)]
+        rim = dot(strips[...], halves(jnp.concatenate(lines, axis=0).astype(BF16))).astype(BF16)
+        to_right[a * 32 : a * 32 + 32, :] = rim[:32]
+        to_left[a * 32 : a * 32 + 32, :] = rim[32:]
+
+
+def rest_kernel(hidden, mixed, wp, mains, main, out):
+    for j in range(BLOCKS):
+        block = slice(j * LANES, j * LANES + LANES)
+        out[:, block] = (hidden[:SENT, block] + dot(mixed[:SENT, :], wp[:, block])).astype(BF16)
     for a in range(N_ROW):
         first = (a + M) % N_ROW
         lines = [out[(8 * k + first) * TW : (8 * k + first + 1) * TW, :] for k in range(4)]
         main[a * 128 : a * 128 + 128, :] = dot(
             mains[...], halves(jnp.concatenate(lines, axis=0))
         ).astype(BF16)
-        lines = [out_side[(8 * k + first) * 8 : (8 * k + first + 1) * 8, :] for k in range(4)]
-        rim = dot(strips[...], halves(jnp.concatenate(lines, axis=0).astype(BF16))).astype(BF16)
-        to_right[a * 32 : a * 32 + 32, :] = rim[:32]
-        to_left[a * 32 : a * 32 + 32, :] = rim[32:]
 
 
 def join_kernel(main, from_left, from_right, out):
@@ -366,7 +411,9 @@
     copy = pltpu.make_async_copy(gathers.at[place[0]], gather, gather_sem)
     copy.start()
     start_block(weights, buffers, sems, 0)
-    group_matrices(buffers[-2], buffers[-1])
+    group_matrices(buffers[-4], buffers[-3])
+    sums = buffers[-2]
+    sums[...] = jnp.zeros_like(sums)
     late = place[1]
     copy.wait()
     for r in range(N_ROW):
@@ -381,13 +428,17 @@
         for h in range(2):
             half = slice(h * D // 2, h * D // 2 + D // 2)
             local[at, half] = value[h * 48 : h * 48 + 48]
-            x_ref[at, half] = value[h * 48 : h * 48 + 48].astype(F32)
-
-    def emit(block, values):
-        dilated = values.astype(BF16).astype(F32)
+            wide = value[h * 48 : h * 48 + 48].astype(F32)
+            x_ref[at, half] = wide
+            add_sums(sums, half, wide)
+
+    refine(TH, False, x_ref, weights, buffers, sems)
+    wp_s, normed = buffers[4:6]
+    for j in range(BLOCKS):
+        block = slice(j * LANES, j * LANES + LANES)
+        value = x_ref[:, block] + dot(normed[...], wp_s[:, block])
+        dilated = value.astype(BF16).astype(F32)
         out[:, block] = (0.6 * local[:, block].astype(F32) + 0.4 * dilated).astype(BF16)
-
-    refine(TH, False, x_ref, weights, buffers, sems, emit)
     for r in range(N_ROW):
         at = slice(r * 48, r * 48 + 48)
         cells = jnp.concatenate([out[at, t * LANES : t * LANES + LANES] for t in range(BLOCKS)], axis=0)
@@ -425,37 +476,56 @@
         pltpu.VMEM((2, 8, 128), F32),
         pltpu.VMEM((D, 128), BF16),
         pltpu.VMEM((128, D), BF16),
+        pltpu.VMEM((16, D), F32),
+        pltpu.VMEM((8, D), F32),
     ]
 
 
 ANY = pl.BlockSpec(memory_space=pl.ANY)
+HBM = pl.BlockSpec(memory_space=pltpu.HBM)
 VMEM = pl.BlockSpec(memory_space=pltpu.VMEM)
-PARAMS = dict(vmem_limit_bytes=56 * 2**20)
+
+
+def params(mib):
+    return pltpu.CompilerParams(vmem_limit_bytes=mib * 2**20)
 
 
 def tile_block(above, own, below, left, right, weights):
     shape = jax.ShapeDtypeStruct
-    return pl.pallas_call(
+    sems, *buffers = scratch(WIN, (WH + 2) * WW)
+    to_left, to_right, hidden, mixed, w_proj = pl.pallas_call(
         tile_kernel,
         out_shape=(
-            shape((2 * SENT, D // 2), BF16),
             shape((2 * STRIP, D // 2), BF16),
             shape((2 * STRIP, D // 2), BF16),
+            shape((WIN, D), F32),
+            shape((WIN, D), BF16),
+            shape((D, D), BF16),
         ),
-        in_specs=[ANY] * 5 + [VMEM] * 3 + [ANY] * 4 + [VMEM, ANY],
-        out_specs=(VMEM, VMEM, VMEM),
+        in_specs=[ANY] * 5 + [VMEM] * 2 + [HBM] * 4 + [VMEM, HBM],
+        out_specs=(VMEM,) * 5,
         scratch_shapes=[
             pltpu.VMEM((SENT, D), BF16),
             pltpu.VMEM((SIDE, D), BF16),
-            pltpu.VMEM((WIN, D), F32),
-            pltpu.VMEM((SENT, D), BF16),
             pltpu.VMEM((SIDE, D), F32),
             pltpu.SemaphoreType.DMA((5,)),
-            *scratch(WIN, (WH + 2) * WW),
+            sems,
+            *buffers[:4],
+            *buffers[6:],
         ],
-        compiler_params=pltpu.CompilerParams(**PARAMS),
+        compiler_params=params(TILE_MIB),
         name="tile_block",
-    )(above, own, below, left, right, side_matrix(), main_matrix(), strip_matrix(), *weights)
+    )(above, own, below, left, right, side_matrix(), strip_matrix(), *weights)
+    main = pl.pallas_call(
+        rest_kernel,
+        out_shape=shape((2 * SENT, D // 2), BF16),
+        in_specs=[VMEM] * 4,
+        out_specs=VMEM,
+        scratch_shapes=[pltpu.VMEM((SENT, D), BF16)],
+        compiler_params=params(REST_MIB),
+        name="rest",
+    )(hidden, mixed, w_proj, main_matrix())
+    return main, to_left, to_right
 
 
 def join(main, from_left, from_right):
@@ -464,6 +534,7 @@
         out_shape=jax.ShapeDtypeStruct(main.shape, BF16),
         in_specs=[VMEM] * 3,
         out_specs=VMEM,
+        compiler_params=params(8),
         name="join",
     )(main, from_left, from_right)
 
@@ -472,7 +543,7 @@
     return pl.pallas_call(
         sub_kernel,
         out_shape=jax.ShapeDtypeStruct((DEV * 8, 2 * LANES), BF16),
-        in_specs=[pl.BlockSpec(memory_space=pltpu.SMEM), VMEM, ANY, VMEM] + [ANY] * 4 + [VMEM, ANY],
+        in_specs=[pl.BlockSpec(memory_space=pltpu.SMEM), VMEM, HBM, VMEM] + [HBM] * 4 + [VMEM, HBM],
         out_specs=VMEM,
         scratch_shapes=[
             pltpu.VMEM((2, 96, 256), BF16),
@@ -482,7 +553,7 @@
             pltpu.SemaphoreType.DMA,
             *scratch(OWN, (TH + 2) * TW),
         ],
-        compiler_params=pltpu.CompilerParams(**PARAMS),
+        compiler_params=params(48),
         name="sub_block",
     )(place, got, gather_matrices(), packing_matrix(), *weights)
 
@@ -493,6 +564,7 @@
         out_shape=jax.ShapeDtypeStruct((OWN, D), BF16),
         in_specs=[VMEM] * 2,
         out_specs=VMEM,
+        compiler_params=params(8),
         name="unpack",
     )(got, packing_matrix())
 

time: 171 us -> 155 us (0.906)
  Pallas kernels: 69.9 us -> 60.2 us
  waiting for transfers between devices: 42.6 us -> 35.9 us
    ppermute x6, waiting for transfers between devices: 21.2 us -> 14 us  [shift(): return lax.ppermute(value, axis, pairs)]
    pallas_call x1, Pallas kernels: 23.6 us -> 19.6 us  [sub_block(): pl.pallas_call(sub_kernel, out_shape=jax.ShapeDtypeStruct((DEV * 8, 2 * L...]
    pallas_call x1 -> x2, Pallas kernels: 41 us -> 37.9 us  [the longest x1 34.9 us: tile_block(): pl.pallas_call(tile_kernel, out_shape=(shape((2 * STRIP, D // 2), BF16),...]
    unnamed x18 -> x20, local copies, waits for them, and re-layouts: 2.63 us -> 4.15 us
  transfers between devices with their start and end apart: 7 -> 7, of which waited for: 7 -> 6; matrix products, arithmetic and copies ran while one was open for 0% -> 0% of each run, Pallas kernels for 0% -> 2%
where the time goes in v2:
time: 155 us
  Pallas kernels  60.2 us (39%)
  waiting for transfers between devices  35.9 us (23%)
  starting transfers between devices  29.5 us (19%)
  blocking collectives  23.5 us (15%)
  local copies, waits for them, and re-layouts  5.68 us (4%)
    pallas_call x1, Pallas kernels, tile_block(): pl.pallas_call(tile_kernel, out_shape=(shape((2 * STRIP, D // 2), BF16),...  34.9 us
    all_to_all x1, blocking collectives, body(): back = both(refined.reshape(DEV, 8, 2 * LANES)).reshape(DEV * 8, 2 * LANES)  23.5 us
    all_to_all x1, waiting for transfers between devices, body(): got = both(main.reshape(DEV, 8, D // 2)).reshape(2 * SENT, D // 2)  21.9 us
    pallas_call x1, Pallas kernels, sub_block(): pl.pallas_call(sub_kernel, out_shape=jax.ShapeDtypeStruct((DEV * 8, 2 * L...  19.6 us
    ppermute x6, starting transfers between devices, shift(): return lax.ppermute(value, axis, pairs)  18.1 us
    ppermute x6, waiting for transfers between devices, shift(): return lax.ppermute(value, axis, pairs)  14 us
    all_to_all x1, starting transfers between devices, body(): got = both(main.reshape(DEV, 8, D // 2)).reshape(2 * SENT, D // 2)  11.4 us
    unnamed x20, local copies, waits for them, and re-layouts  4.15 us
  transfers between devices with their start and end apart: 7, of which 6 were waited for; matrix products, arithmetic and copies ran while one was open for 0% of the time, Pallas kernels for 2%

profile of v2, /device:TPU:1, one launch (start us, length us, event | category | flops | bytes accessed | tf_op | source)
XLA Modules:
  0.0 155.0 jit_solution(16938077940061849508)
XLA Ops:
  0.0 1.1 fusion.1
  1.1 4.0 %collective-permute-start = (bf16[4,16,1280]{2,1,0:T(8,128)(2,1)S(1)}, bf16[4,16,1280]{2,1,0:T(8,128)(2,1)S(1)}, u32[]{:S(2)}, u32[]{:S(2)}) collective-permute-start(bf16[4,16,1280]{2,1,0:T(8,128)(2,1)S(1)} %get-tuple-element.18), channel_id=1, source_target_pairs={{0,16},{16,32},{32,48},{48,64},{64,80},{80,96},{96,112},{1,17},{17... | collective-permute-start | bytes 491528 | tf_op jit(solution)/shard_map/ppermute | solution.py:575
  5.1 1.3 collective-permute-start.1
  6.4 1.5 collective-permute-done
  8.0 3.7 %collective-permute-done.1 = bf16[4,16,1280]{2,1,0:T(8,128)(2,1)S(1)} collective-permute-done((bf16[4,16,1280]{2,1,0:T(8,128)(2,1)S(1)}, bf16[4,16,1280]{2,1,0:T(8,128)(2,1)S(1)}, u32[]{:S(2)}, u32[]{:S(2)}) %collective-permute-start.1) | collective-permute-done | bytes 163872 | tf_op jit(solution)/shard_map/ppermute | solution.py:575
  11.8 0.3 fusion
  12.0 0.1 reshape.33
  12.1 6.6 %collective-permute-start.2 = (bf16[128,1280]{1,0:T(8,128)(2,1)S(1)}, bf16[128,1280]{1,0:T(8,128)(2,1)S(1)}, u32[]{:S(2)}, u32[]{:S(2)}) collective-permute-start(bf16[128,1280]{1,0:T(8,128)(2,1)S(1)} %reshape.33), channel_id=1, source_target_pairs={{0,1},{1,2},{2,3},{3,4},{4,5},{5,6},{6,7},{7,8},{8,9},{9,10},{10,1... | collective-permute-start | bytes 983048 | tf_op jit(solution)/shard_map/ppermute | solution.py:575
  18.8 1.9 %collective-permute-start.3 = (bf16[128,1280]{1,0:T(8,128)(2,1)S(1)}, bf16[128,1280]{1,0:T(8,128)(2,1)S(1)}, u32[]{:S(2)}, u32[]{:S(2)}) collective-permute-start(bf16[128,1280]{1,0:T(8,128)(2,1)S(1)} %reshape.34), channel_id=1, source_target_pairs={{1,0},{2,1},{3,2},{4,3},{5,4},{6,5},{7,6},{8,7},{9,8},{10,9},{11,1... | collective-permute-start | bytes 983048 | tf_op jit(solution)/shard_map/ppermute | solution.py:575
  20.7 2.0 %collective-permute-done.2.left = bf16[128,1280]{1,0:T(8,128)(2,1)S(1)} collective-permute-done((bf16[128,1280]{1,0:T(8,128)(2,1)S(1)}, bf16[128,1280]{1,0:T(8,128)(2,1)S(1)}, u32[]{:S(2)}, u32[]{:S(2)}) %collective-permute-start.2) | collective-permute-done | bytes 327712 | tf_op jit(solution)/shard_map/ppermute | solution.py:575
  22.7 6.0 %collective-permute-done.3.right = bf16[128,1280]{1,0:T(8,128)(2,1)S(1)} collective-permute-done((bf16[128,1280]{1,0:T(8,128)(2,1)S(1)}, bf16[128,1280]{1,0:T(8,128)(2,1)S(1)}, u32[]{:S(2)}, u32[]{:S(2)}) %collective-permute-start.3) | collective-permute-done | bytes 327712 | tf_op jit(solution)/shard_map/ppermute | solution.py:575
  28.7 34.9 %tile_block.1 = (bf16[256,640]{1,0:T(8,128)(2,1)S(1)}, bf16[256,640]{1,0:T(8,128)(2,1)S(1)}, f32[768,1280]{1,0:T(8,128)}, bf16[768,1280]{1,0:T(8,128)(2,1)S(1)}, bf16[1280,1280]{1,0:T(8,128)(2,1)}) custom-call(bf16[64,1280]{1,0:T(8,128)(2,1)S(1)} %bitcast.14, bf16[384,1280]{1,0:T(8,128)(2,1)S(1)} %bitcast.10, bf16[64,1280]{1,0:T(8,128)(2,1)S(1)} %bitcast.15, ...), custom_call_target="tpu_custom_call" | custom-call | tf_op jit(solution)/shard_map/tile_block/pallas_call | solution.py:496
  63.6 1.9 %collective-permute-start.4 = (bf16[256,640]{1,0:T(8,128)(2,1)S(1)}, bf16[256,640]{1,0:T(8,128)(2,1)S(1)}, u32[]{:S(2)}, u32[]{:S(2)}) collective-permute-start(bf16[256,640]{1,0:T(8,128)(2,1)S(1)} %get-tuple-element.13), channel_id=1, source_target_pairs={{0,1},{1,2},{2,3},{3,4},{4,5},{5,6},{6,7},{7,8},{8,9},{9,10},{10,1... | collective-permute-start | bytes 983048 | tf_op jit(solution)/shard_map/ppermute | solution.py:575
  65.5 2.4 %collective-permute-start.5 = (bf16[256,640]{1,0:T(8,128)(2,1)S(1)}, bf16[256,640]{1,0:T(8,128)(2,1)S(1)}, u32[]{:S(2)}, u32[]{:S(2)}) collective-permute-start(bf16[256,640]{1,0:T(8,128)(2,1)S(1)} %get-tuple-element.14), channel_id=1, source_target_pairs={{1,0},{2,1},{3,2},{4,3},{5,4},{6,5},{7,6},{8,7},{9,8},{10,9},{11,1... | collective-permute-start | bytes 983048 | tf_op jit(solution)/shard_map/ppermute | solution.py:575
  68.0 2.1 %copy-done.1 = f32[768,1280]{1,0:T(8,128)S(1)} copy-done((f32[768,1280]{1,0:T(8,128)S(1)}, f32[768,1280]{1,0:T(8,128)}, u32[]{:S(2)}) %copy-start.1) | copy-done | bytes 3932184
  70.1 1.9 %copy-done.2 = bf16[1280,1280]{1,0:T(8,128)(2,1)S(1)} copy-done((bf16[1280,1280]{1,0:T(8,128)(2,1)S(1)}, bf16[1280,1280]{1,0:T(8,128)(2,1)}, u32[]{:S(2)}) %copy-start.2) | copy-done | bytes 3276824
  72.0 2.9 %rest.1.main = bf16[1024,640]{1,0:T(8,128)(2,1)S(1)} custom-call(f32[768,1280]{1,0:T(8,128)S(1)} %copy-done.1, bf16[768,1280]{1,0:T(8,128)(2,1)S(1)} %get-tuple-element.11.mixed, bf16[1280,1280]{1,0:T(8,128)(2,1)S(1)} %copy-done.2, bf16[128,128]{1,0:T(8,128)(2,1)S(1)} %copy-done.7), custom_call_target="tpu_custom_call" | custom-call | tf_op jit(solution)/shard_map/rest/pallas_call | solution.py:519
  75.0 0.8 collective-permute-done.5.from_right
  75.8 1.2 join.1
  77.0 11.4 %all-to-all-start = ((bf16[128,8,640]{2,1,0:T(8,128)(2,1)}), bf16[128,8,640]{2,1,0:T(8,128)(2,1)S(1)}, u32[]{:S(2)}, u32[]{:S(2)}) async-start(bf16[128,8,640]{2,1,0:T(8,128)(2,1)} %bitcast.5), calls=%async_computation | async-start | bytes 2621440 | tf_op jit(solution)/shard_map/all_to_all | solution.py:597
  88.6 21.9 %all-to-all-done = bf16[128,8,640]{2,1,0:T(8,128)(2,1)S(1)} async-done(((bf16[128,8,640]{2,1,0:T(8,128)(2,1)}), bf16[128,8,640]{2,1,0:T(8,128)(2,1)S(1)}, u32[]{:S(2)}, u32[]{:S(2)}) %all-to-all-start) | async-done | bytes 1310752 | tf_op jit(solution)/shard_map/all_to_all | solution.py:597
  110.4 19.6 %sub_block.1 = bf16[1024,512]{1,0:T(8,128)(2,1)S(1)} custom-call(s32[2]{0:T(128)S(1)} %pad_add_fusion.place, bf16[1024,640]{1,0:T(8,128)(2,1)S(1)} %bitcast.11, bf16[6,2,96,256]{3,2,1,0:T(8,128)(2,1)S(1)} %copy-done.3, bf16[256,240]{1,0:T(8,128)(2,1)S(1)} %copy-done.4, bf16[1280,1280]{1,0:T(8,128)(2,1)} %wq.3, bf16[1280,1280]{1,0:T(8,128)(2,1)} %wk.3, ...), custom_call_target="tpu_custom_call" | custom-call | tf_op jit(solution)/shard_map/sub_block/pallas_call | solution.py:543
  130.1 23.5 %all_to_all.10 = bf16[128,8,512]{2,1,0:T(8,128)(2,1)S(1)} all-to-all(bf16[128,8,512]{2,1,0:T(8,128)(2,1)S(1)} %bitcast.12), channel_id=1, replica_groups=mesh['row'=8,'col'=16] {'row','col'}, dimensions={0} | all-to-all | bytes 2097152 | tf_op jit(solution)/shard_map/all_to_all | solution.py:599
  153.6 1.4 unpack.1
  (22 shorter events, 0.3 us)
Async XLA Ops:
  0.0 7.9 %copy-start = (bf16[24,16,1280]{2,1,0:T(8,128)(2,1)S(1)}, bf16[24,16,1280]{2,1,0:T(8,128)(2,1)}, u32[]{:S(2)}) copy-start(bf16[24,16,1280]{2,1,0:T(8,128)(2,1)} %param.13) | copy-start | bytes 2949124
  1.1 6.8 %collective-permute-start = (bf16[4,16,1280]{2,1,0:T(8,128)(2,1)S(1)}, bf16[4,16,1280]{2,1,0:T(8,128)(2,1)S(1)}, u32[]{:S(2)}, u32[]{:S(2)}) collective-permute-start(bf16[4,16,1280]{2,1,0:T(8,128)(2,1)S(1)} %get-tuple-element.18), channel_id=1, source_target_pairs={{0,16},{16,32},{32,48},{48,64},{64,80},{80,96},{96,112},{1,17},{17... | collective-permute-start | bytes 491528 | tf_op jit(solution)/shard_map/ppermute | solution.py:575
  5.1 6.6 %collective-permute-start.1 = (bf16[4,16,1280]{2,1,0:T(8,128)(2,1)S(1)}, bf16[4,16,1280]{2,1,0:T(8,128)(2,1)S(1)}, u32[]{:S(2)}, u32[]{:S(2)}) collective-permute-start(bf16[4,16,1280]{2,1,0:T(8,128)(2,1)S(1)} %get-tuple-element.17), channel_id=1, source_target_pairs={{16,0},{32,16},{48,32},{64,48},{80,64},{96,80},{112,96},{17,1},{33... | collective-permute-start | bytes 491528 | tf_op jit(solution)/shard_map/ppermute | solution.py:575
  11.7 17.0 %copy-start.5 = (f32[9,1280]{1,0:T(8,128)S(1)}, f32[9,1280]{1,0:T(8,128)}, u32[]{:S(2)}) copy-start(f32[9,1280]{1,0:T(8,128)} %taps.3) | copy-start | bytes 138244
  11.7 16.9 %copy-start.6 = (bf16[256,256]{1,0:T(8,128)(2,1)S(1)}, bf16[256,256]{1,0:T(8,128)(2,1)}, u32[]{:S(2)}) copy-start(bf16[256,256]{1,0:T(8,128)(2,1)} %constant.27.clone.sides) | copy-start | bytes 393220
  11.8 16.9 %copy-start.8 = (bf16[64,64]{1,0:T(8,128)(2,1)S(1)}, bf16[64,64]{1,0:T(8,128)(2,1)}, u32[]{:S(2)}) copy-start(bf16[64,64]{1,0:T(8,128)(2,1)} %constant.28.clone.strips) | copy-start | bytes 24580
  12.1 10.6 %collective-permute-start.2 = (bf16[128,1280]{1,0:T(8,128)(2,1)S(1)}, bf16[128,1280]{1,0:T(8,128)(2,1)S(1)}, u32[]{:S(2)}, u32[]{:S(2)}) collective-permute-start(bf16[128,1280]{1,0:T(8,128)(2,1)S(1)} %reshape.33), channel_id=1, source_target_pairs={{0,1},{1,2},{2,3},{3,4},{4,5},{5,6},{6,7},{7,8},{8,9},{9,10},{10,1... | collective-permute-start | bytes 983048 | tf_op jit(solution)/shard_map/ppermute | solution.py:575
  18.8 9.9 %collective-permute-start.3 = (bf16[128,1280]{1,0:T(8,128)(2,1)S(1)}, bf16[128,1280]{1,0:T(8,128)(2,1)S(1)}, u32[]{:S(2)}, u32[]{:S(2)}) collective-permute-start(bf16[128,1280]{1,0:T(8,128)(2,1)S(1)} %reshape.34), channel_id=1, source_target_pairs={{1,0},{2,1},{3,2},{4,3},{5,4},{6,5},{7,6},{8,7},{9,8},{10,9},{11,1... | collective-permute-start | bytes 983048 | tf_op jit(solution)/shard_map/ppermute | solution.py:575
  28.7 39.3 %copy-start.7 = (bf16[128,128]{1,0:T(8,128)(2,1)S(1)}, bf16[128,128]{1,0:T(8,128)(2,1)}, u32[]{:S(2)}) copy-start(bf16[128,128]{1,0:T(8,128)(2,1)} %constant.29.clone.mains) | copy-start | bytes 98308
  63.6 11.4 %collective-permute-start.4 = (bf16[256,640]{1,0:T(8,128)(2,1)S(1)}, bf16[256,640]{1,0:T(8,128)(2,1)S(1)}, u32[]{:S(2)}, u32[]{:S(2)}) collective-permute-start(bf16[256,640]{1,0:T(8,128)(2,1)S(1)} %get-tuple-element.13), channel_id=1, source_target_pairs={{0,1},{1,2},{2,3},{3,4},{4,5},{5,6},{6,7},{7,8},{8,9},{9,10},{10,1... | collective-permute-start | bytes 983048 | tf_op jit(solution)/shard_map/ppermute | solution.py:575
  65.5 10.3 %collective-permute-start.5 = (bf16[256,640]{1,0:T(8,128)(2,1)S(1)}, bf16[256,640]{1,0:T(8,128)(2,1)S(1)}, u32[]{:S(2)}, u32[]{:S(2)}) collective-permute-start(bf16[256,640]{1,0:T(8,128)(2,1)S(1)} %get-tuple-element.14), channel_id=1, source_target_pairs={{1,0},{2,1},{3,2},{4,3},{5,4},{6,5},{7,6},{8,7},{9,8},{10,9},{11,1... | collective-permute-start | bytes 983048 | tf_op jit(solution)/shard_map/ppermute | solution.py:575
  68.0 2.1 %copy-start.1 = (f32[768,1280]{1,0:T(8,128)S(1)}, f32[768,1280]{1,0:T(8,128)}, u32[]{:S(2)}) copy-start(f32[768,1280]{1,0:T(8,128)} %get-tuple-element.10.hidden) | copy-start | bytes 11796484
  70.1 1.9 %copy-start.2 = (bf16[1280,1280]{1,0:T(8,128)(2,1)S(1)}, bf16[1280,1280]{1,0:T(8,128)(2,1)}, u32[]{:S(2)}) copy-start(bf16[1280,1280]{1,0:T(8,128)(2,1)} %get-tuple-element.12.wp) | copy-start | bytes 9830404
  77.0 33.4 %copy-start.3 = (bf16[6,2,96,256]{3,2,1,0:T(8,128)(2,1)S(1)}, bf16[6,2,96,256]{3,2,1,0:T(8,128)(2,1)}, u32[]{:S(2)}) copy-start(bf16[6,2,96,256]{3,2,1,0:T(8,128)(2,1)} %constant.30.clone.gathers) | copy-start | bytes 1769476
  77.0 33.4 %copy-start.4 = (bf16[256,240]{1,0:T(8,128)(2,1)S(1)}, bf16[256,240]{1,0:T(8,128)(2,1)}, u32[]{:S(2)}) copy-start(bf16[256,240]{1,0:T(8,128)(2,1)} %constant.31.clone.packing) | copy-start | bytes 368644
  77.0 33.4 %all-to-all-start = ((bf16[128,8,640]{2,1,0:T(8,128)(2,1)}), bf16[128,8,640]{2,1,0:T(8,128)(2,1)S(1)}, u32[]{:S(2)}, u32[]{:S(2)}) async-start(bf16[128,8,640]{2,1,0:T(8,128)(2,1)} %bitcast.5), calls=%async_computation | async-start | bytes 2621440 | tf_op jit(solution)/shard_map/all_to_all | solution.py:597

commit v3 on v2

--- a/solution.py
+++ b/solution.py
@@ -33,7 +33,7 @@
 BF16 = jnp.bfloat16
 HIGH_SUM = 2.0**100
 LOW_SUM = 2.0**-100
-TILE_MIB = 48
+TILE_MIB = 46
 REST_MIB = 14
 
 

time: 155 us -> 154 us (level)
  local copies, waits for them, and re-layouts: 5.68 us -> 3.75 us
  waiting for transfers between devices: 35.9 us -> 37.8 us
    ppermute x6, waiting for transfers between devices: 14 us -> 16 us  [shift(): return lax.ppermute(value, axis, pairs)]
    unnamed x20 -> x18, local copies, waits for them, and re-layouts: 4.15 us -> 2.22 us
where the time goes in v3:
time: 154 us
  Pallas kernels  59.1 us (38%)
  waiting for transfers between devices  37.8 us (25%)
  starting transfers between devices  29.5 us (19%)
  blocking collectives  23.5 us (15%)
  local copies, waits for them, and re-layouts  3.75 us (2%)
    pallas_call x1, Pallas kernels, tile_block(): pl.pallas_call(tile_kernel, out_shape=(shape((2 * STRIP, D // 2), BF16),...  33.9 us
    all_to_all x1, blocking collectives, body(): back = both(refined.reshape(DEV, 8, 2 * LANES)).reshape(DEV * 8, 2 * LANES)  23.5 us
    all_to_all x1, waiting for transfers between devices, body(): got = both(main.reshape(DEV, 8, D // 2)).reshape(2 * SENT, D // 2)  21.9 us
    pallas_call x1, Pallas kernels, sub_block(): pl.pallas_call(sub_kernel, out_shape=jax.ShapeDtypeStruct((DEV * 8, 2 * L...  19.6 us
    ppermute x6, starting transfers between devices, shift(): return lax.ppermute(value, axis, pairs)  18.1 us
    ppermute x6, waiting for transfers between devices, shift(): return lax.ppermute(value, axis, pairs)  16 us
    all_to_all x1, starting transfers between devices, body(): got = both(main.reshape(DEV, 8, D // 2)).reshape(2 * SENT, D // 2)  11.4 us
  transfers between devices with their start and end apart: 7, of which 6 were waited for; matrix products, arithmetic and copies ran while one was open for 0% of the time, Pallas kernels for 2%

profile of v3, /device:TPU:1, one launch (start us, length us, event | category | flops | bytes accessed | tf_op | source)
XLA Modules:
  0.0 154.0 jit_solution(5883140900862801373)
XLA Ops:
  0.0 1.1 fusion.1
  1.1 4.0 %collective-permute-start = (bf16[4,16,1280]{2,1,0:T(8,128)(2,1)S(1)}, bf16[4,16,1280]{2,1,0:T(8,128)(2,1)S(1)}, u32[]{:S(2)}, u32[]{:S(2)}) collective-permute-start(bf16[4,16,1280]{2,1,0:T(8,128)(2,1)S(1)} %get-tuple-element.18), channel_id=1, source_target_pairs={{0,16},{16,32},{32,48},{48,64},{64,80},{80,96},{96,112},{1,17},{17... | collective-permute-start | bytes 491528 | tf_op jit(solution)/shard_map/ppermute | solution.py:575
  5.1 1.3 collective-permute-start.1
  6.4 1.5 %collective-permute-done = bf16[4,16,1280]{2,1,0:T(8,128)(2,1)S(1)} collective-permute-done((bf16[4,16,1280]{2,1,0:T(8,128)(2,1)S(1)}, bf16[4,16,1280]{2,1,0:T(8,128)(2,1)S(1)}, u32[]{:S(2)}, u32[]{:S(2)}) %collective-permute-start) | collective-permute-done | bytes 163872 | tf_op jit(solution)/shard_map/ppermute | solution.py:575
  8.0 3.7 %collective-permute-done.1 = bf16[4,16,1280]{2,1,0:T(8,128)(2,1)S(1)} collective-permute-done((bf16[4,16,1280]{2,1,0:T(8,128)(2,1)S(1)}, bf16[4,16,1280]{2,1,0:T(8,128)(2,1)S(1)}, u32[]{:S(2)}, u32[]{:S(2)}) %collective-permute-start.1) | collective-permute-done | bytes 163872 | tf_op jit(solution)/shard_map/ppermute | solution.py:575
  11.8 0.3 fusion
  12.0 0.1 reshape.33
  12.1 6.6 %collective-permute-start.2 = (bf16[128,1280]{1,0:T(8,128)(2,1)S(1)}, bf16[128,1280]{1,0:T(8,128)(2,1)S(1)}, u32[]{:S(2)}, u32[]{:S(2)}) collective-permute-start(bf16[128,1280]{1,0:T(8,128)(2,1)S(1)} %reshape.33), channel_id=1, source_target_pairs={{0,1},{1,2},{2,3},{3,4},{4,5},{5,6},{6,7},{7,8},{8,9},{9,10},{10,1... | collective-permute-start | bytes 983048 | tf_op jit(solution)/shard_map/ppermute | solution.py:575
  18.7 0.1 reshape.34
  18.8 1.9 %collective-permute-start.3 = (bf16[128,1280]{1,0:T(8,128)(2,1)S(1)}, bf16[128,1280]{1,0:T(8,128)(2,1)S(1)}, u32[]{:S(2)}, u32[]{:S(2)}) collective-permute-start(bf16[128,1280]{1,0:T(8,128)(2,1)S(1)} %reshape.34), channel_id=1, source_target_pairs={{1,0},{2,1},{3,2},{4,3},{5,4},{6,5},{7,6},{8,7},{9,8},{10,9},{11,1... | collective-permute-start | bytes 983048 | tf_op jit(solution)/shard_map/ppermute | solution.py:575
  20.7 2.0 %collective-permute-done.2.left = bf16[128,1280]{1,0:T(8,128)(2,1)S(1)} collective-permute-done((bf16[128,1280]{1,0:T(8,128)(2,1)S(1)}, bf16[128,1280]{1,0:T(8,128)(2,1)S(1)}, u32[]{:S(2)}, u32[]{:S(2)}) %collective-permute-start.2) | collective-permute-done | bytes 327712 | tf_op jit(solution)/shard_map/ppermute | solution.py:575
  22.7 6.0 %collective-permute-done.3.right = bf16[128,1280]{1,0:T(8,128)(2,1)S(1)} collective-permute-done((bf16[128,1280]{1,0:T(8,128)(2,1)S(1)}, bf16[128,1280]{1,0:T(8,128)(2,1)S(1)}, u32[]{:S(2)}, u32[]{:S(2)}) %collective-permute-start.3) | collective-permute-done | bytes 327712 | tf_op jit(solution)/shard_map/ppermute | solution.py:575
  28.7 33.9 %tile_block.1 = (bf16[256,640]{1,0:T(8,128)(2,1)S(1)}, bf16[256,640]{1,0:T(8,128)(2,1)S(1)}, f32[768,1280]{1,0:T(8,128)}, bf16[768,1280]{1,0:T(8,128)(2,1)S(1)}, bf16[1280,1280]{1,0:T(8,128)(2,1)S(1)}) custom-call(bf16[64,1280]{1,0:T(8,128)(2,1)S(1)} %bitcast.14, bf16[384,1280]{1,0:T(8,128)(2,1)S(1)} %bitcast.10, bf16[64,1280]{1,0:T(8,128)(2,1)S(1)} %bitcast.15, ...), custom_call_target="tpu_custom_call" | custom-call | tf_op jit(solution)/shard_map/tile_block/pallas_call | solution.py:496
  62.6 1.9 %collective-permute-start.4 = (bf16[256,640]{1,0:T(8,128)(2,1)S(1)}, bf16[256,640]{1,0:T(8,128)(2,1)S(1)}, u32[]{:S(2)}, u32[]{:S(2)}) collective-permute-start(bf16[256,640]{1,0:T(8,128)(2,1)S(1)} %get-tuple-element.13), channel_id=1, source_target_pairs={{0,1},{1,2},{2,3},{3,4},{4,5},{5,6},{6,7},{7,8},{8,9},{9,10},{10,1... | collective-permute-start | bytes 983048 | tf_op jit(solution)/shard_map/ppermute | solution.py:575
  64.5 2.4 %collective-permute-start.5 = (bf16[256,640]{1,0:T(8,128)(2,1)S(1)}, bf16[256,640]{1,0:T(8,128)(2,1)S(1)}, u32[]{:S(2)}, u32[]{:S(2)}) collective-permute-start(bf16[256,640]{1,0:T(8,128)(2,1)S(1)} %get-tuple-element.14), channel_id=1, source_target_pairs={{1,0},{2,1},{3,2},{4,3},{5,4},{6,5},{7,6},{8,7},{9,8},{10,9},{11,1... | collective-permute-start | bytes 983048 | tf_op jit(solution)/shard_map/ppermute | solution.py:575
  67.0 2.1 %copy-done.1 = f32[768,1280]{1,0:T(8,128)S(1)} copy-done((f32[768,1280]{1,0:T(8,128)S(1)}, f32[768,1280]{1,0:T(8,128)}, u32[]{:S(2)}) %copy-start.1) | copy-done | bytes 3932184
  69.1 2.9 %rest.1.main = bf16[1024,640]{1,0:T(8,128)(2,1)S(1)} custom-call(f32[768,1280]{1,0:T(8,128)S(1)} %copy-done.1, bf16[768,1280]{1,0:T(8,128)(2,1)S(1)} %get-tuple-element.11.mixed, bf16[1280,1280]{1,0:T(8,128)(2,1)S(1)} %get-tuple-element.12.wp, bf16[128,128]{1,0:T(8,128)(2,1)S(1)} %copy-done.6), custom_call_target="tpu_custom_call" | custom-call | tf_op jit(solution)/shard_map/rest/pallas_call | solution.py:519
  72.0 2.7 %collective-permute-done.5.from_right = bf16[256,640]{1,0:T(8,128)(2,1)S(1)} collective-permute-done((bf16[256,640]{1,0:T(8,128)(2,1)S(1)}, bf16[256,640]{1,0:T(8,128)(2,1)S(1)}, u32[]{:S(2)}, u32[]{:S(2)}) %collective-permute-start.5) | collective-permute-done | bytes 327712 | tf_op jit(solution)/shard_map/ppermute | solution.py:575
  74.8 1.2 join.1
  76.0 11.4 %all-to-all-start = ((bf16[128,8,640]{2,1,0:T(8,128)(2,1)}), bf16[128,8,640]{2,1,0:T(8,128)(2,1)S(1)}, u32[]{:S(2)}, u32[]{:S(2)}) async-start(bf16[128,8,640]{2,1,0:T(8,128)(2,1)} %bitcast.5), calls=%async_computation | async-start | bytes 2621440 | tf_op jit(solution)/shard_map/all_to_all | solution.py:597
  87.6 21.9 %all-to-all-done = bf16[128,8,640]{2,1,0:T(8,128)(2,1)S(1)} async-done(((bf16[128,8,640]{2,1,0:T(8,128)(2,1)}), bf16[128,8,640]{2,1,0:T(8,128)(2,1)S(1)}, u32[]{:S(2)}, u32[]{:S(2)}) %all-to-all-start) | async-done | bytes 1310752 | tf_op jit(solution)/shard_map/all_to_all | solution.py:597
  109.4 19.6 %sub_block.1 = bf16[1024,512]{1,0:T(8,128)(2,1)S(1)} custom-call(s32[2]{0:T(128)S(1)} %pad_add_fusion.place, bf16[1024,640]{1,0:T(8,128)(2,1)S(1)} %bitcast.11, bf16[6,2,96,256]{3,2,1,0:T(8,128)(2,1)S(1)} %copy-done.2, bf16[256,240]{1,0:T(8,128)(2,1)S(1)} %copy-done.3, bf16[1280,1280]{1,0:T(8,128)(2,1)} %wq.3, bf16[1280,1280]{1,0:T(8,128)(2,1)} %wk.3, ...), custom_call_target="tpu_custom_call" | custom-call | tf_op jit(solution)/shard_map/sub_block/pallas_call | solution.py:543
  129.1 23.5 %all_to_all.10 = bf16[128,8,512]{2,1,0:T(8,128)(2,1)S(1)} all-to-all(bf16[128,8,512]{2,1,0:T(8,128)(2,1)S(1)} %bitcast.12), channel_id=1, replica_groups=mesh['row'=8,'col'=16] {'row','col'}, dimensions={0} | all-to-all | bytes 2097152 | tf_op jit(solution)/shard_map/all_to_all | solution.py:599
  152.6 1.4 unpack.1
  (20 shorter events, 0.2 us)
Async XLA Ops:
  0.0 7.9 %copy-start = (bf16[24,16,1280]{2,1,0:T(8,128)(2,1)S(1)}, bf16[24,16,1280]{2,1,0:T(8,128)(2,1)}, u32[]{:S(2)}) copy-start(bf16[24,16,1280]{2,1,0:T(8,128)(2,1)} %param.13) | copy-start | bytes 2949124
  1.1 6.8 %collective-permute-start = (bf16[4,16,1280]{2,1,0:T(8,128)(2,1)S(1)}, bf16[4,16,1280]{2,1,0:T(8,128)(2,1)S(1)}, u32[]{:S(2)}, u32[]{:S(2)}) collective-permute-start(bf16[4,16,1280]{2,1,0:T(8,128)(2,1)S(1)} %get-tuple-element.18), channel_id=1, source_target_pairs={{0,16},{16,32},{32,48},{48,64},{64,80},{80,96},{96,112},{1,17},{17... | collective-permute-start | bytes 491528 | tf_op jit(solution)/shard_map/ppermute | solution.py:575
  5.1 6.6 %collective-permute-start.1 = (bf16[4,16,1280]{2,1,0:T(8,128)(2,1)S(1)}, bf16[4,16,1280]{2,1,0:T(8,128)(2,1)S(1)}, u32[]{:S(2)}, u32[]{:S(2)}) collective-permute-start(bf16[4,16,1280]{2,1,0:T(8,128)(2,1)S(1)} %get-tuple-element.17), channel_id=1, source_target_pairs={{16,0},{32,16},{48,32},{64,48},{80,64},{96,80},{112,96},{17,1},{33... | collective-permute-start | bytes 491528 | tf_op jit(solution)/shard_map/ppermute | solution.py:575
  11.7 17.0 %copy-start.4 = (f32[9,1280]{1,0:T(8,128)S(1)}, f32[9,1280]{1,0:T(8,128)}, u32[]{:S(2)}) copy-start(f32[9,1280]{1,0:T(8,128)} %taps.3) | copy-start | bytes 138244
  11.7 16.9 %copy-start.5 = (bf16[256,256]{1,0:T(8,128)(2,1)S(1)}, bf16[256,256]{1,0:T(8,128)(2,1)}, u32[]{:S(2)}) copy-start(bf16[256,256]{1,0:T(8,128)(2,1)} %constant.27.clone.sides) | copy-start | bytes 393220
  11.8 16.9 %copy-start.7 = (bf16[64,64]{1,0:T(8,128)(2,1)S(1)}, bf16[64,64]{1,0:T(8,128)(2,1)}, u32[]{:S(2)}) copy-start(bf16[64,64]{1,0:T(8,128)(2,1)} %constant.28.clone.strips) | copy-start | bytes 24580
  12.1 10.6 %collective-permute-start.2 = (bf16[128,1280]{1,0:T(8,128)(2,1)S(1)}, bf16[128,1280]{1,0:T(8,128)(2,1)S(1)}, u32[]{:S(2)}, u32[]{:S(2)}) collective-permute-start(bf16[128,1280]{1,0:T(8,128)(2,1)S(1)} %reshape.33), channel_id=1, source_target_pairs={{0,1},{1,2},{2,3},{3,4},{4,5},{5,6},{6,7},{7,8},{8,9},{9,10},{10,1... | collective-permute-start | bytes 983048 | tf_op jit(solution)/shard_map/ppermute | solution.py:575
  18.8 9.9 %collective-permute-start.3 = (bf16[128,1280]{1,0:T(8,128)(2,1)S(1)}, bf16[128,1280]{1,0:T(8,128)(2,1)S(1)}, u32[]{:S(2)}, u32[]{:S(2)}) collective-permute-start(bf16[128,1280]{1,0:T(8,128)(2,1)S(1)} %reshape.34), channel_id=1, source_target_pairs={{1,0},{2,1},{3,2},{4,3},{5,4},{6,5},{7,6},{8,7},{9,8},{10,9},{11,1... | collective-permute-start | bytes 983048 | tf_op jit(solution)/shard_map/ppermute | solution.py:575
  28.7 38.3 %copy-start.6 = (bf16[128,128]{1,0:T(8,128)(2,1)S(1)}, bf16[128,128]{1,0:T(8,128)(2,1)}, u32[]{:S(2)}) copy-start(bf16[128,128]{1,0:T(8,128)(2,1)} %constant.29.clone.mains) | copy-start | bytes 98308
  62.6 9.4 %collective-permute-start.4 = (bf16[256,640]{1,0:T(8,128)(2,1)S(1)}, bf16[256,640]{1,0:T(8,128)(2,1)S(1)}, u32[]{:S(2)}, u32[]{:S(2)}) collective-permute-start(bf16[256,640]{1,0:T(8,128)(2,1)S(1)} %get-tuple-element.13), channel_id=1, source_target_pairs={{0,1},{1,2},{2,3},{3,4},{4,5},{5,6},{6,7},{7,8},{8,9},{9,10},{10,1... | collective-permute-start | bytes 983048 | tf_op jit(solution)/shard_map/ppermute | solution.py:575
  64.5 10.3 %collective-permute-start.5 = (bf16[256,640]{1,0:T(8,128)(2,1)S(1)}, bf16[256,640]{1,0:T(8,128)(2,1)S(1)}, u32[]{:S(2)}, u32[]{:S(2)}) collective-permute-start(bf16[256,640]{1,0:T(8,128)(2,1)S(1)} %get-tuple-element.14), channel_id=1, source_target_pairs={{1,0},{2,1},{3,2},{4,3},{5,4},{6,5},{7,6},{8,7},{9,8},{10,9},{11,1... | collective-permute-start | bytes 983048 | tf_op jit(solution)/shard_map/ppermute | solution.py:575
  67.0 2.1 %copy-start.1 = (f32[768,1280]{1,0:T(8,128)S(1)}, f32[768,1280]{1,0:T(8,128)}, u32[]{:S(2)}) copy-start(f32[768,1280]{1,0:T(8,128)} %get-tuple-element.10.hidden) | copy-start | bytes 11796484
  76.0 33.4 %copy-start.2 = (bf16[6,2,96,256]{3,2,1,0:T(8,128)(2,1)S(1)}, bf16[6,2,96,256]{3,2,1,0:T(8,128)(2,1)}, u32[]{:S(2)}) copy-start(bf16[6,2,96,256]{3,2,1,0:T(8,128)(2,1)} %constant.30.clone.gathers) | copy-start | bytes 1769476
  76.0 33.4 %copy-start.3 = (bf16[256,240]{1,0:T(8,128)(2,1)S(1)}, bf16[256,240]{1,0:T(8,128)(2,1)}, u32[]{:S(2)}) copy-start(bf16[256,240]{1,0:T(8,128)(2,1)} %constant.31.clone.packing) | copy-start | bytes 368644
  76.0 33.4 %all-to-all-start = ((bf16[128,8,640]{2,1,0:T(8,128)(2,1)}), bf16[128,8,640]{2,1,0:T(8,128)(2,1)S(1)}, u32[]{:S(2)}, u32[]{:S(2)}) async-start(bf16[128,8,640]{2,1,0:T(8,128)(2,1)} %bitcast.5), calls=%async_computation | async-start | bytes 2621440 | tf_op jit(solution)/shard_map/all_to_all | solution.py:597

commit v4 on v3

--- a/solution.py
+++ b/solution.py
@@ -390,7 +390,7 @@
         ).astype(BF16)
 
 
-def join_kernel(main, from_left, from_right, out):
+def join_kernel(place, main, from_left, from_right, out):
     for a in range(N_ROW):
         first, last = a * 128, a * 128 + 96
         rim = slice(a * 32, a * 32 + 32)
@@ -528,15 +528,15 @@
     return main, to_left, to_right
 
 
-def join(main, from_left, from_right):
+def join(place, main, from_left, from_right):
     return pl.pallas_call(
         join_kernel,
         out_shape=jax.ShapeDtypeStruct(main.shape, BF16),
-        in_specs=[VMEM] * 3,
+        in_specs=[pl.BlockSpec(memory_space=pltpu.SMEM)] + [VMEM] * 3,
         out_specs=VMEM,
         compiler_params=params(8),
         name="join",
-    )(main, from_left, from_right)
+    )(place, main, from_left, from_right)
 
 
 def sub_block(place, got, weights):
@@ -590,7 +590,7 @@
         above.reshape(M * TW, D), latent.reshape(OWN, D), below.reshape(M * TW, D),
         left, right, weights,
     )
-    main = join(main, shift(to_right, "col", 1), shift(to_left, "col", -1))
+    main = join(place, main, shift(to_right, "col", 1), shift(to_left, "col", -1))
     both = functools.partial(
         lax.all_to_all, axis_name=("row", "col"), split_axis=0, concat_axis=0, tiled=True
     )

time: 154 us -> 158 us (1.026)
  blocking collectives: 23.5 us -> 56.7 us
  waiting for transfers between devices: 37.8 us -> 13.4 us
  starting transfers between devices: 29.5 us -> 18.1 us
  local copies, waits for them, and re-layouts: 3.75 us -> 9.09 us
    all_to_all x0 -> x1, blocking collectives: none -> 33.2 us  [body(): got = both(main.reshape(DEV, 8, D // 2)).reshape(2 * SENT, D // 2)]
    all_to_all x1 -> x0, waiting for transfers between devices: 21.9 us -> none  [body(): got = both(main.reshape(DEV, 8, D // 2)).reshape(2 * SENT, D // 2)]
    all_to_all x1 -> x0, starting transfers between devices: 11.4 us -> none  [body(): got = both(main.reshape(DEV, 8, D // 2)).reshape(2 * SENT, D // 2)]
    unnamed x18 -> x26, local copies, waits for them, and re-layouts: 2.22 us -> 7.56 us
    ppermute x6, waiting for transfers between devices: 16 us -> 13.4 us  [shift(): return lax.ppermute(value, axis, pairs)]
    pallas_call x1, Pallas kernels: 33.9 us -> 35.7 us  [tile_block(): pl.pallas_call(tile_kernel, out_shape=(shape((2 * STRIP, D // 2), BF16),...]
  transfers between devices with their start and end apart: 7 -> 6, of which waited for: 6 -> 5; matrix products, arithmetic and copies ran while one was open for 0% -> 0% of each run, Pallas kernels for 2% -> 2%
where the time goes in v4:
time: 158 us
  Pallas kernels  60.4 us (38%)
  blocking collectives  56.7 us (36%)
  starting transfers between devices  18.1 us (11%)
  waiting for transfers between devices  13.4 us (8%)
  local copies, waits for them, and re-layouts  9.09 us (6%)
    pallas_call x1, Pallas kernels, tile_block(): pl.pallas_call(tile_kernel, out_shape=(shape((2 * STRIP, D // 2), BF16),...  35.7 us
    all_to_all x1, blocking collectives, body(): got = both(main.reshape(DEV, 8, D // 2)).reshape(2 * SENT, D // 2)  33.2 us
    all_to_all x1, blocking collectives, body(): back = both(refined.reshape(DEV, 8, 2 * LANES)).reshape(DEV * 8, 2 * LANES)  23.5 us
    pallas_call x1, Pallas kernels, sub_block(): pl.pallas_call(sub_kernel, out_shape=jax.ShapeDtypeStruct((DEV * 8, 2 * L...  19.7 us
    ppermute x6, starting transfers between devices, shift(): return lax.ppermute(value, axis, pairs)  18.1 us
    ppermute x6, waiting for transfers between devices, shift(): return lax.ppermute(value, axis, pairs)  13.4 us
    unnamed x26, local copies, waits for them, and re-layouts  7.56 us
  transfers between devices with their start and end apart: 6, of which 5 were waited for; matrix products, arithmetic and copies ran while one was open for 0% of the time, Pallas kernels for 2%

profile of v4, /device:TPU:1, one launch (start us, length us, event | category | flops | bytes accessed | tf_op | source)
XLA Modules:
  0.0 158.0 jit_solution(568445127534154661)
XLA Ops:
  0.0 1.1 fusion.1
  1.1 4.0 %collective-permute-start = (bf16[4,16,1280]{2,1,0:T(8,128)(2,1)S(1)}, bf16[4,16,1280]{2,1,0:T(8,128)(2,1)S(1)}, u32[]{:S(2)}, u32[]{:S(2)}) collective-permute-start(bf16[4,16,1280]{2,1,0:T(8,128)(2,1)S(1)} %get-tuple-element.18), channel_id=1, source_target_pairs={{0,16},{16,32},{32,48},{48,64},{64,80},{80,96},{96,112},{1,17},{17... | collective-permute-start | bytes 491528 | tf_op jit(solution)/shard_map/ppermute | solution.py:575
  5.1 1.3 collective-permute-start.1
  6.4 1.5 collective-permute-done
  8.0 3.7 %collective-permute-done.1 = bf16[4,16,1280]{2,1,0:T(8,128)(2,1)S(1)} collective-permute-done((bf16[4,16,1280]{2,1,0:T(8,128)(2,1)S(1)}, bf16[4,16,1280]{2,1,0:T(8,128)(2,1)S(1)}, u32[]{:S(2)}, u32[]{:S(2)}) %collective-permute-start.1) | collective-permute-done | bytes 163872 | tf_op jit(solution)/shard_map/ppermute | solution.py:575
  12.1 6.6 %collective-permute-start.2 = (bf16[128,1280]{1,0:T(8,128)(2,1)S(1)}, bf16[128,1280]{1,0:T(8,128)(2,1)S(1)}, u32[]{:S(2)}, u32[]{:S(2)}) collective-permute-start(bf16[128,1280]{1,0:T(8,128)(2,1)S(1)} %reshape.33), channel_id=1, source_target_pairs={{0,1},{1,2},{2,3},{3,4},{4,5},{5,6},{6,7},{7,8},{8,9},{9,10},{10,1... | collective-permute-start | bytes 983048 | tf_op jit(solution)/shard_map/ppermute | solution.py:575
  18.8 1.9 %collective-permute-start.3 = (bf16[128,1280]{1,0:T(8,128)(2,1)S(1)}, bf16[128,1280]{1,0:T(8,128)(2,1)S(1)}, u32[]{:S(2)}, u32[]{:S(2)}) collective-permute-start(bf16[128,1280]{1,0:T(8,128)(2,1)S(1)} %reshape.34), channel_id=1, source_target_pairs={{1,0},{2,1},{3,2},{4,3},{5,4},{6,5},{7,6},{8,7},{9,8},{10,9},{11,1... | collective-permute-start | bytes 983048 | tf_op jit(solution)/shard_map/ppermute | solution.py:575
  20.7 2.0 %collective-permute-done.2.left = bf16[128,1280]{1,0:T(8,128)(2,1)S(1)} collective-permute-done((bf16[128,1280]{1,0:T(8,128)(2,1)S(1)}, bf16[128,1280]{1,0:T(8,128)(2,1)S(1)}, u32[]{:S(2)}, u32[]{:S(2)}) %collective-permute-start.2) | collective-permute-done | bytes 327712 | tf_op jit(solution)/shard_map/ppermute | solution.py:575
  22.7 0.7 copy-done.7
  23.4 5.3 %collective-permute-done.3.right = bf16[128,1280]{1,0:T(8,128)(2,1)S(1)} collective-permute-done((bf16[128,1280]{1,0:T(8,128)(2,1)S(1)}, bf16[128,1280]{1,0:T(8,128)(2,1)S(1)}, u32[]{:S(2)}, u32[]{:S(2)}) %collective-permute-start.3) | collective-permute-done | bytes 327712 | tf_op jit(solution)/shard_map/ppermute | solution.py:575
  28.7 1.0 copy-done.8
  29.7 35.7 %tile_block.1 = (bf16[256,640]{1,0:T(8,128)(2,1)}, bf16[256,640]{1,0:T(8,128)(2,1)}, f32[768,1280]{1,0:T(8,128)}, bf16[768,1280]{1,0:T(8,128)(2,1)S(1)}, bf16[1280,1280]{1,0:T(8,128)(2,1)S(1)}) custom-call(bf16[64,1280]{1,0:T(8,128)(2,1)S(1)} %bitcast.15, bf16[384,1280]{1,0:T(8,128)(2,1)S(1)} %bitcast.10, bf16[64,1280]{1,0:T(8,128)(2,1)S(1)} %bitcast.16, ...), custom_call_target="tpu_custom_call" | custom-call | tf_op jit(solution)/shard_map/tile_block/pallas_call | solution.py:496
  65.4 1.7 %copy-done.2 = bf16[1280,1280]{1,0:T(8,128)(2,1)} copy-done((bf16[1280,1280]{1,0:T(8,128)(2,1)}, bf16[1280,1280]{1,0:T(8,128)(2,1)S(1)}, u32[]{:S(2)}) %copy-start.2) | copy-done | bytes 3276824
  67.1 1.9 %collective-permute-start.4 = (bf16[256,640]{1,0:T(8,128)(2,1)}, bf16[256,640]{1,0:T(8,128)(2,1)S(1)}, u32[]{:S(2)}, u32[]{:S(2)}) collective-permute-start(bf16[256,640]{1,0:T(8,128)(2,1)} %get-tuple-element.13), channel_id=1, source_target_pairs={{0,1},{1,2},{2,3},{3,4},{4,5},{5,6},{6,7},{7,8},{8,9},{9,10},{10,1... | collective-permute-start | bytes 983048 | tf_op jit(solution)/shard_map/ppermute | solution.py:575
  69.0 2.4 %collective-permute-start.5 = (bf16[256,640]{1,0:T(8,128)(2,1)}, bf16[256,640]{1,0:T(8,128)(2,1)S(1)}, u32[]{:S(2)}, u32[]{:S(2)}) collective-permute-start(bf16[256,640]{1,0:T(8,128)(2,1)} %get-tuple-element.14), channel_id=1, source_target_pairs={{1,0},{2,1},{3,2},{4,3},{5,4},{6,5},{7,6},{8,7},{9,8},{10,9},{11,1... | collective-permute-start | bytes 983048 | tf_op jit(solution)/shard_map/ppermute | solution.py:575
  71.5 2.1 %copy-done.1 = f32[768,1280]{1,0:T(8,128)S(1)} copy-done((f32[768,1280]{1,0:T(8,128)S(1)}, f32[768,1280]{1,0:T(8,128)}, u32[]{:S(2)}) %copy-start.1) | copy-done | bytes 3932184
  73.7 1.9 %copy-done.3 = bf16[1280,1280]{1,0:T(8,128)(2,1)S(1)} copy-done((bf16[1280,1280]{1,0:T(8,128)(2,1)S(1)}, bf16[1280,1280]{1,0:T(8,128)(2,1)}, u32[]{:S(2)}) %copy-start.3) | copy-done | bytes 3276824
  75.6 2.9 %rest.1.main = bf16[1024,640]{1,0:T(8,128)(2,1)S(1)} custom-call(f32[768,1280]{1,0:T(8,128)S(1)} %copy-done.1, bf16[768,1280]{1,0:T(8,128)(2,1)S(1)} %get-tuple-element.11.mixed, bf16[1280,1280]{1,0:T(8,128)(2,1)S(1)} %copy-done.3, bf16[128,128]{1,0:T(8,128)(2,1)S(1)} %copy-done.10), custom_call_target="tpu_custom_call" | custom-call | tf_op jit(solution)/shard_map/rest/pallas_call | solution.py:519
  78.5 0.9 collective-permute-done.5.from_right
  79.5 0.7 join.1
  80.2 33.2 %all_to_all.10 = bf16[128,8,640]{2,1,0:T(8,128)(2,1)S(1)} all-to-all(bf16[128,8,640]{2,1,0:T(8,128)(2,1)S(1)} %bitcast.12), channel_id=1, replica_groups=mesh['row'=8,'col'=16] {'row','col'}, dimensions={0} | all-to-all | bytes 2621440 | tf_op jit(solution)/shard_map/all_to_all | solution.py:597
  113.4 19.7 %sub_block.1 = bf16[1024,512]{1,0:T(8,128)(2,1)S(1)} custom-call(s32[2]{0:T(128)S(1)} %pad_add_fusion.place, bf16[1024,640]{1,0:T(8,128)(2,1)S(1)} %bitcast.11, bf16[6,2,96,256]{3,2,1,0:T(8,128)(2,1)S(1)} %copy-done.4, bf16[256,240]{1,0:T(8,128)(2,1)S(1)} %copy-done.5, bf16[1280,1280]{1,0:T(8,128)(2,1)} %wq.3, bf16[1280,1280]{1,0:T(8,128)(2,1)} %wk.3, ...), custom_call_target="tpu_custom_call" | custom-call | tf_op jit(solution)/shard_map/sub_block/pallas_call | solution.py:543
  133.1 23.5 %all_to_all.11 = bf16[128,8,512]{2,1,0:T(8,128)(2,1)S(1)} all-to-all(bf16[128,8,512]{2,1,0:T(8,128)(2,1)S(1)} %bitcast.13), channel_id=1, replica_groups=mesh['row'=8,'col'=16] {'row','col'}, dimensions={0} | all-to-all | bytes 2097152 | tf_op jit(solution)/shard_map/all_to_all | solution.py:599
  156.6 1.4 unpack.1
  (27 shorter events, 0.6 us)
Async XLA Ops:
  0.0 7.9 %copy-start = (bf16[24,16,1280]{2,1,0:T(8,128)(2,1)S(1)}, bf16[24,16,1280]{2,1,0:T(8,128)(2,1)}, u32[]{:S(2)}) copy-start(bf16[24,16,1280]{2,1,0:T(8,128)(2,1)} %param.13) | copy-start | bytes 2949124
  1.1 6.8 %collective-permute-start = (bf16[4,16,1280]{2,1,0:T(8,128)(2,1)S(1)}, bf16[4,16,1280]{2,1,0:T(8,128)(2,1)S(1)}, u32[]{:S(2)}, u32[]{:S(2)}) collective-permute-start(bf16[4,16,1280]{2,1,0:T(8,128)(2,1)S(1)} %get-tuple-element.18), channel_id=1, source_target_pairs={{0,16},{16,32},{32,48},{48,64},{64,80},{80,96},{96,112},{1,17},{17... | collective-permute-start | bytes 491528 | tf_op jit(solution)/shard_map/ppermute | solution.py:575
  5.1 6.6 %collective-permute-start.1 = (bf16[4,16,1280]{2,1,0:T(8,128)(2,1)S(1)}, bf16[4,16,1280]{2,1,0:T(8,128)(2,1)S(1)}, u32[]{:S(2)}, u32[]{:S(2)}) collective-permute-start(bf16[4,16,1280]{2,1,0:T(8,128)(2,1)S(1)} %get-tuple-element.17), channel_id=1, source_target_pairs={{16,0},{32,16},{48,32},{64,48},{80,64},{96,80},{112,96},{17,1},{33... | collective-permute-start | bytes 491528 | tf_op jit(solution)/shard_map/ppermute | solution.py:575
  11.7 17.0 %copy-start.6 = (f32[9,1280]{1,0:T(8,128)S(1)}, f32[9,1280]{1,0:T(8,128)}, u32[]{:S(2)}) copy-start(f32[9,1280]{1,0:T(8,128)} %taps.3) | copy-start | bytes 138244
  11.7 16.9 %copy-start.9 = (bf16[256,256]{1,0:T(8,128)(2,1)S(1)}, bf16[256,256]{1,0:T(8,128)(2,1)}, u32[]{:S(2)}) copy-start(bf16[256,256]{1,0:T(8,128)(2,1)} %constant.27.clone.sides) | copy-start | bytes 393220
  11.8 16.9 %copy-start.11 = (bf16[64,64]{1,0:T(8,128)(2,1)S(1)}, bf16[64,64]{1,0:T(8,128)(2,1)}, u32[]{:S(2)}) copy-start(bf16[64,64]{1,0:T(8,128)(2,1)} %constant.28.clone.strips) | copy-start | bytes 24580
  12.1 10.6 %collective-permute-start.2 = (bf16[128,1280]{1,0:T(8,128)(2,1)S(1)}, bf16[128,1280]{1,0:T(8,128)(2,1)S(1)}, u32[]{:S(2)}, u32[]{:S(2)}) collective-permute-start(bf16[128,1280]{1,0:T(8,128)(2,1)S(1)} %reshape.33), channel_id=1, source_target_pairs={{0,1},{1,2},{2,3},{3,4},{4,5},{5,6},{6,7},{7,8},{8,9},{9,10},{10,1... | collective-permute-start | bytes 983048 | tf_op jit(solution)/shard_map/ppermute | solution.py:575
  18.8 9.9 %collective-permute-start.3 = (bf16[128,1280]{1,0:T(8,128)(2,1)S(1)}, bf16[128,1280]{1,0:T(8,128)(2,1)S(1)}, u32[]{:S(2)}, u32[]{:S(2)}) collective-permute-start(bf16[128,1280]{1,0:T(8,128)(2,1)S(1)} %reshape.34), channel_id=1, source_target_pairs={{1,0},{2,1},{3,2},{4,3},{5,4},{6,5},{7,6},{8,7},{9,8},{10,9},{11,1... | collective-permute-start | bytes 983048 | tf_op jit(solution)/shard_map/ppermute | solution.py:575
  22.7 0.7 copy-start.7
  28.7 1.0 copy-start.8
  29.7 41.9 %copy-start.10 = (bf16[128,128]{1,0:T(8,128)(2,1)S(1)}, bf16[128,128]{1,0:T(8,128)(2,1)}, u32[]{:S(2)}) copy-start(bf16[128,128]{1,0:T(8,128)(2,1)} %constant.29.clone.mains) | copy-start | bytes 98308
  65.4 1.7 %copy-start.2 = (bf16[1280,1280]{1,0:T(8,128)(2,1)}, bf16[1280,1280]{1,0:T(8,128)(2,1)S(1)}, u32[]{:S(2)}) copy-start(bf16[1280,1280]{1,0:T(8,128)(2,1)S(1)} %get-tuple-element.12.wp) | copy-start | bytes 9830404
  67.1 11.4 %collective-permute-start.4 = (bf16[256,640]{1,0:T(8,128)(2,1)}, bf16[256,640]{1,0:T(8,128)(2,1)S(1)}, u32[]{:S(2)}, u32[]{:S(2)}) collective-permute-start(bf16[256,640]{1,0:T(8,128)(2,1)} %get-tuple-element.13), channel_id=1, source_target_pairs={{0,1},{1,2},{2,3},{3,4},{4,5},{5,6},{6,7},{7,8},{8,9},{9,10},{10,1... | collective-permute-start | bytes 983048 | tf_op jit(solution)/shard_map/ppermute | solution.py:575
  69.0 10.5 %collective-permute-start.5 = (bf16[256,640]{1,0:T(8,128)(2,1)}, bf16[256,640]{1,0:T(8,128)(2,1)S(1)}, u32[]{:S(2)}, u32[]{:S(2)}) collective-permute-start(bf16[256,640]{1,0:T(8,128)(2,1)} %get-tuple-element.14), channel_id=1, source_target_pairs={{1,0},{2,1},{3,2},{4,3},{5,4},{6,5},{7,6},{8,7},{9,8},{10,9},{11,1... | collective-permute-start | bytes 983048 | tf_op jit(solution)/shard_map/ppermute | solution.py:575
  71.5 2.1 %copy-start.1 = (f32[768,1280]{1,0:T(8,128)S(1)}, f32[768,1280]{1,0:T(8,128)}, u32[]{:S(2)}) copy-start(f32[768,1280]{1,0:T(8,128)} %get-tuple-element.10.hidden) | copy-start | bytes 11796484
  73.7 1.9 %copy-start.3 = (bf16[1280,1280]{1,0:T(8,128)(2,1)S(1)}, bf16[1280,1280]{1,0:T(8,128)(2,1)}, u32[]{:S(2)}) copy-start(bf16[1280,1280]{1,0:T(8,128)(2,1)} %copy-done.2) | copy-start | bytes 9830404
  80.2 33.2 %copy-start.4 = (bf16[6,2,96,256]{3,2,1,0:T(8,128)(2,1)S(1)}, bf16[6,2,96,256]{3,2,1,0:T(8,128)(2,1)}, u32[]{:S(2)}) copy-start(bf16[6,2,96,256]{3,2,1,0:T(8,128)(2,1)} %constant.30.clone.gathers) | copy-start | bytes 1769476
  80.2 33.2 %copy-start.5 = (bf16[256,240]{1,0:T(8,128)(2,1)S(1)}, bf16[256,240]{1,0:T(8,128)(2,1)}, u32[]{:S(2)}) copy-start(bf16[256,240]{1,0:T(8,128)(2,1)} %constant.31.clone.packing) | copy-start | bytes 368644
